TPU v7x, 256 devices: a whole 4x4x8 slice. The times are simulated.
256 devices in a mesh: section: 64 (over x, y, z_hi, core), tp: 4 (over z_lo).
Axes of the slice: x: 4, y: 4, z: 8 (z_hi: 2, z_lo: 4; z = z_hi * 4 + z_lo), core: 2. Of those that a mesh axis runs over, the one named last changes fastest.
Arguments:
- queries: bfloat16 [24576, 6144], P('section', 'tp'), may hold values from -60 to 60
- keys: bfloat16 [24576, 6144], P('section', 'tp'), may hold values from -6 to 6
- values: bfloat16 [24576, 6144], P('section', 'tp'), may hold values from -40 to 40
- cotangent: bfloat16 [24576, 6144], P('section', 'tp'), may hold values from -6 to 6
- doc_ids: int32 [24576], P('section'), may hold values from 0 to 15, never falling along the last dimension, each value on 1 to 3072 neighbouring positions
- gain: float32 [6144], P('tp'), may hold values from 0.1 to 1.9
Outputs:
- normed: bfloat16 [24576, 6144], P('section', 'tp')
- grad_queries: bfloat16 [24576, 6144], P('section', 'tp')
- grad_keys: bfloat16 [24576, 6144], P('section', 'tp')
- grad_values: bfloat16 [24576, 6144], P('section', 'tp')
All inputs are finite; a program needn't handle non-finite values.
Results may differ from a plain program's by a relative error of at most 0.009.
Values may be sent and summed in bfloat16 or wider, within the bound.
No kernel may reach another device: no remote copies, remote signals or barrier semaphores. Data moves between devices by JAX's collectives and lax.ppermute only.
A program may use at most 192 MiB of HBM per device.

v0:
```python
import jax
import jax.numpy as jnp
from jax import lax
from jax.sharding import PartitionSpec as P

HS = 128
BAND_DEV = 2


def from_behind(value, axis, steps):
    count = lax.axis_size(axis)
    initial, last = (max(0, -steps), min(count, count - steps))
    return lax.ppermute(value, axis, [(source, source + steps) for source in range(initial, last)])


def band_mask(query_pos, query_doc, key_pos, key_doc, window):
    distance = query_pos[:, None] - key_pos[None, :]
    return (
        (distance >= 0)
        & (distance < window)
        & (key_pos[None, :] >= 0)
        & (query_doc[:, None] == key_doc[None, :])
    )


def body(queries, keys, values, cotangent, doc_ids, gain):
    tok_rows = queries.shape[0]
    head_count = queries.shape[1] // HS
    feature_total = queries.shape[1] * lax.axis_size("tp")
    section_index = lax.axis_index("section")
    window = BAND_DEV * tok_rows
    score_scale = HS ** (-0.5)
    offsets = jnp.arange(tok_rows, dtype=jnp.int32)
    own_pos = section_index * tok_rows + offsets
    query_heads = queries.reshape(tok_rows, head_count, HS)
    blocks = [(keys, values, doc_ids)]
    current = (keys, values, doc_ids)
    for distance in range(1, BAND_DEV + 1):
        current = from_behind((current[0], current[1], current[2]), "section", 1)
        blocks.append(current)
    key_band = jnp.concatenate([entry[0] for entry in blocks], 0).reshape(-1, head_count, HS)
    value_band = jnp.concatenate([entry[1] for entry in blocks], 0).reshape(-1, head_count, HS)
    doc_band = jnp.concatenate([entry[2] for entry in blocks], 0)
    key_pos = jnp.concatenate(
        [(section_index - distance) * tok_rows + offsets for distance in range(BAND_DEV + 1)], 0
    )
    visible = band_mask(own_pos, doc_ids, key_pos, doc_band, window)
    scores = (
        jnp.einsum("qhd,khd->hqk", query_heads, key_band, preferred_element_type=jnp.float32)
        * score_scale
    )
    scores = jnp.where(visible[None], scores, -1e30)
    row_max = jnp.max(scores, axis=-1, keepdims=True)
    log_total = row_max + jnp.log(jnp.sum(jnp.exp(scores - row_max), axis=-1, keepdims=True))
    weights = jnp.exp(scores - log_total)
    weights_b = weights.astype(jnp.bfloat16)
    attended = jnp.einsum(
        "hqk,khd->qhd", weights_b, value_band, preferred_element_type=jnp.float32
    ).reshape(tok_rows, -1)
    squares = lax.psum(jnp.sum(attended * attended, axis=-1), "tp")
    inverse = lax.rsqrt(squares / feature_total + 1e-05)[:, None]
    normed = (attended * inverse * gain).astype(jnp.bfloat16)
    scaled_grad = cotangent.astype(jnp.float32) * gain
    inner_sum = lax.psum(jnp.sum(scaled_grad * attended, axis=-1), "tp")[:, None]
    grad_out = (inverse * scaled_grad - attended * inverse**3 * inner_sum / feature_total).astype(
        jnp.bfloat16
    )
    grad_heads = grad_out.reshape(tok_rows, head_count, HS)
    row_delta = jnp.sum(
        grad_heads.astype(jnp.float32) * attended.reshape(tok_rows, head_count, HS), axis=-1
    ).T
    grad_weights = jnp.einsum(
        "qhd,khd->hqk", grad_heads, value_band, preferred_element_type=jnp.float32
    )
    dscore = (weights * (grad_weights - row_delta[:, :, None])).astype(jnp.bfloat16)
    grad_query = (
        jnp.einsum("hqk,khd->qhd", dscore, key_band, preferred_element_type=jnp.float32)
        * score_scale
    )
    key_terms = (
        jnp.einsum("hqk,qhd->khd", dscore, query_heads, preferred_element_type=jnp.float32)
        * score_scale
    ).reshape(-1, queries.shape[1])
    value_terms = jnp.einsum(
        "hqk,qhd->khd", weights_b, grad_heads, preferred_element_type=jnp.float32
    ).reshape(-1, queries.shape[1])
    grad_key = key_terms[:tok_rows]
    grad_value = value_terms[:tok_rows]
    for distance in range(1, BAND_DEV + 1):
        partial_value = (
            key_terms[distance * tok_rows : (distance + 1) * tok_rows],
            value_terms[distance * tok_rows : (distance + 1) * tok_rows],
        )
        arrived = from_behind((partial_value[0], partial_value[1]), "section", -distance)
        grad_key = grad_key + arrived[0]
        grad_value = grad_value + arrived[1]
    return (
        normed,
        grad_query.reshape(tok_rows, -1).astype(jnp.bfloat16),
        grad_key.astype(jnp.bfloat16),
        grad_value.astype(jnp.bfloat16),
    )


def solution(mesh):
    return jax.shard_map(
        body,
        mesh=mesh,
        in_specs=(
            P("section", "tp"),
            P("section", "tp"),
            P("section", "tp"),
            P("section", "tp"),
            P("section"),
            P("tp"),
        ),
        out_specs=(P("section", "tp"), P("section", "tp"), P("section", "tp"), P("section", "tp")),
        check_vma=False,
    )
```

profile of v0, /device:TPU:5, one launch (start us, length us, event | category | flops | bytes accessed | tf_op | source)
XLA Modules:
  0.0 531.6 jit_solution(1407093929953470929)
XLA Ops:
  0.7 9.5 %collective-permute-start = (bf16[384,1536]{1,0:T(8,128)(2,1)}, bf16[384,1536]{1,0:T(8,128)(2,1)S(1)}, u32[]{:S(2)}, u32[]{:S(2)}) collective-permute-start(bf16[384,1536]{1,0:T(8,128)(2,1)} %param.8), channel_id=1, source_target_pairs={{0,4},{4,8},{8,12},{12,16},{16,20},{20,24},{24,28},{28,32},{32,36}... | collective-permute-start | bytes 3538952 | tf_op jit(solution)/shard_map/ppermute | solution.py:13
  13.8 13.3 %collective-permute-done = bf16[384,1536]{1,0:T(8,128)(2,1)S(1)} collective-permute-done((bf16[384,1536]{1,0:T(8,128)(2,1)}, bf16[384,1536]{1,0:T(8,128)(2,1)S(1)}, u32[]{:S(2)}, u32[]{:S(2)}) %collective-permute-start) | collective-permute-done | bytes 1179680 | tf_op jit(solution)/shard_map/ppermute | solution.py:13
  27.1 8.2 %collective-permute-start.1 = (bf16[384,1536]{1,0:T(8,128)(2,1)S(1)}, bf16[384,1536]{1,0:T(8,128)(2,1)}, u32[]{:S(2)}, u32[]{:S(2)}) collective-permute-start(bf16[384,1536]{1,0:T(8,128)(2,1)S(1)} %collective-permute-done), channel_id=1, source_target_pairs={{0,4},{4,8},{8,12},{12,16},{16,20},{20,24},{24,28},{28,32},{32,36}... | collective-permute-start | bytes 3538952 | tf_op jit(solution)/shard_map/ppermute | solution.py:13
  37.3 49.7 %collective-permute-done.2 = s32[384]{0:T(512)} collective-permute-done((s32[384]{0:T(512)S(1)}, s32[384]{0:T(512)}, u32[]{:S(2)}, u32[]{:S(2)}) %collective-permute-start.2) | collective-permute-done | bytes 1568 | tf_op jit(solution)/shard_map/ppermute | solution.py:13
  87.0 8.4 %collective-permute-start.3 = (s32[384]{0:T(512)}, s32[384]{0:T(512)}, u32[]{:S(2)}, u32[]{:S(2)}) collective-permute-start(s32[384]{0:T(512)} %collective-permute-done.2), channel_id=1, source_target_pairs={{0,4},{4,8},{8,12},{12,16},{16,20},{20,24},{24,28},{28,32},{32,36}... | collective-permute-start | bytes 4616 | tf_op jit(solution)/shard_map/ppermute | solution.py:13
  100.0 2.9 fusion.8
  105.0 3.9 copy.32
  108.9 13.1 %collective-permute-done.5 = bf16[384,1536]{0,1:T(8,128)(2,1)} collective-permute-done((bf16[384,1536]{0,1:T(8,128)(2,1)}, bf16[384,1536]{0,1:T(8,128)(2,1)}, u32[]{:S(2)}, u32[]{:S(2)}) %collective-permute-start.5) | collective-permute-done | bytes 1179680 | tf_op jit(solution)/shard_map/ppermute | solution.py:13
  124.2 9.2 %fusion.11 = (f32[12,384]{1,0:T(8,128)S(1)}, f32[12,384,1152]{1,2,0:T(8,128)}) fusion(bf16[1152,12,128]{0,2,1:T(8,128)(2,1)S(1)} %bitcast.39, bf16[384,12,128]{0,2,1:T(8,128)(2,1)S(1)} %bitcast.48, pred[384,1152]{0,1:T(8,128)(4,1)S(1)} %copy-done.5), kind=kOutput, calls=%fused_computation.37 | convolution fusion | flops 1374875136 | bytes 26413056 | tf_op jit(solution)/shard_map/qhd,khd->hqk/dot_general | solution.py:49
  133.4 9.0 %exponential_reduce_fusion = f32[12,384]{1,0:T(8,128)S(1)} fusion(f32[12,384,1152]{1,2,0:T(8,128)} %get-tuple-element.25, f32[12,384]{1,0:T(8,128)S(1)} %get-tuple-element.24), kind=kLoop, calls=%fused_computation.3 | loop fusion | flops 10612224 | bytes 21270528 | tf_op jit(solution)/shard_map/reduce_sum | solution.py:54
  142.4 11.9 %fusion.5 = (f32[384]{0:T(512)S(1)}, f32[12,128,384]{2,1,0:T(8,128)}) fusion(bf16[1152,12,128]{0,2,1:T(8,128)(2,1)S(1)} %bitcast.42, f32[12,384,1152]{1,2,0:T(8,128)} %get-tuple-element.25, f32[12,384]{1,0:T(8,128)S(1)} %log_add_fusion), kind=kOutput, calls=%fused_computation.15 | convolution fusion | flops 1370750592 | bytes 27151872 | tf_op jit(solution)/shard_map/hqk,khd->qhd/dot_general | solution.py:57
  154.3 3.1 copy.39
  159.8 8.7 %all-reduce = (f32[384]{0:T(512)}, f32[384]{0:T(512)}) all-reduce(f32[384]{0:T(512)S(1)} %get-tuple-element.26, f32[384]{0:T(512)S(1)} %multiply_reduce_fusion), channel_id=1, replica_groups=mesh['section'=64,'tp'=4] {'tp'}, use_global_device_ids=true, to_apply=%region_3.4 | all-reduce | flops 768 | bytes 6144 | tf_op jit(solution)/shard_map/psum | solution.py:60
  169.2 4.4 subtract_convert_fusion
  178.3 16.1 %multiply_convert_fusion = bf16[12,384,1152]{1,2,0:T(8,128)(2,1)} fusion(bf16[384,12,128]{0,2,1:T(8,128)(2,1)S(1)} %bitcast.46, bf16[1152,12,128]{0,2,1:T(8,128)(2,1)} %bitcast.41, f32[12,384,1152]{1,2,0:T(8,128)} %get-tuple-element.25, f32[12,384]{1,0:T(8,128)S(1)} %bitcast.56, f32[12,384]{1,0:T(8,128)S(1)} %copy-done.9), kind=kOutput, calls=%fused_computation.1 | convolution fusion | flops 1380188160 | bytes 36605952 | tf_op jit(solution)/shard_map/qhd,khd->hqk/dot_general | solution.py:72
  194.4 10.8 %multiply_bitcast_fusion = f32[1152,12,128]{0,2,1:T(8,128)} fusion(bf16[12,384,1152]{1,2,0:T(8,128)(2,1)} %multiply_convert_fusion, bf16[384,12,128]{0,2,1:T(8,128)(2,1)} %bitcast.47), kind=kOutput, calls=%fused_computation.5 | convolution fusion | flops 1360723968 | bytes 18874368 | tf_op jit(solution)/shard_map/hqk,qhd->khd/dot_general | solution.py:81
  205.2 6.2 %fusion.10 = (f32[384,12,128]{0,2,1:T(8,128)}, f32[384,12,128]{0,2,1:T(8,128)}, f32[384,12,128]{0,2,1:T(8,128)}) fusion(f32[1152,12,128]{0,2,1:T(8,128)} %multiply_bitcast_fusion), kind=kLoop, calls=%fused_computation.36 | loop fusion | bytes 14155776 | tf_op jit(solution)/shard_map/slice | solution.py:91
  211.3 3.1 copy.50
  214.4 9.9 %collective-permute-start.7 = (f32[384,1536]{1,0:T(8,128)}, f32[384,1536]{1,0:T(8,128)}, u32[]{:S(2)}, u32[]{:S(2)}) collective-permute-start(f32[384,1536]{1,0:T(8,128)} %copy.50), channel_id=1, source_target_pairs={{8,0},{12,4},{16,8},{20,12},{24,16},{28,20},{32,24},{36,28},{40,32... | collective-permute-start | bytes 7077896 | tf_op jit(solution)/shard_map/ppermute | solution.py:13
  224.3 3.1 copy.48
  227.5 8.1 %collective-permute-start.6 = (f32[384,1536]{1,0:T(8,128)}, f32[384,1536]{1,0:T(8,128)}, u32[]{:S(2)}, u32[]{:S(2)}) collective-permute-start(f32[384,1536]{1,0:T(8,128)} %copy.48), channel_id=1, source_target_pairs={{4,0},{8,4},{12,8},{16,12},{20,16},{24,20},{28,24},{32,28},{36,32}... | collective-permute-start | bytes 7077896 | tf_op jit(solution)/shard_map/ppermute | solution.py:13
  235.5 13.9 %convolution_bitcast_fusion = f32[1152,12,128]{0,2,1:T(8,128)} fusion(bf16[384,12,128]{0,2,1:T(8,128)(2,1)} %bitcast.45, f32[12,384,1152]{1,2,0:T(8,128)} %get-tuple-element.25, f32[12,384]{1,0:T(8,128)} %copy-done.8), kind=kOutput, calls=%fused_computation.6 | convolution fusion | flops 1369571328 | bytes 29509632 | tf_op jit(solution)/shard_map/hqk,qhd->khd/dot_general | solution.py:84
  249.4 6.1 %fusion.9 = (f32[384,12,128]{0,2,1:T(8,128)}, f32[384,12,128]{0,2,1:T(8,128)}, f32[384,12,128]{0,2,1:T(8,128)}) fusion(f32[1152,12,128]{0,2,1:T(8,128)} %convolution_bitcast_fusion), kind=kLoop, calls=%fused_computation.35 | loop fusion | bytes 14155776 | tf_op jit(solution)/shard_map/slice | solution.py:92
  255.5 3.1 copy.54
  260.5 3.1 copy.52
  265.7 7.2 %multiply_convert_fusion.1 = bf16[12,128,384]{2,1,0:T(8,128)(2,1)} fusion(bf16[1152,12,128]{0,2,1:T(8,128)(2,1)S(1)} %bitcast.40, bf16[12,384,1152]{1,2,0:T(8,128)(2,1)} %multiply_convert_fusion), kind=kOutput, calls=%fused_computation.18 | convolution fusion | flops 1360134144 | bytes 15335424 | tf_op jit(solution)/shard_map/hqk,khd->qhd/dot_general | solution.py:77
  272.9 2.5 copy.55
  279.5 64.6 %collective-permute-done.7 = f32[384,1536]{1,0:T(8,128)} collective-permute-done((f32[384,1536]{1,0:T(8,128)}, f32[384,1536]{1,0:T(8,128)}, u32[]{:S(2)}, u32[]{:S(2)}) %collective-permute-start.7) | collective-permute-done | bytes 2359328 | tf_op jit(solution)/shard_map/ppermute | solution.py:13
  344.0 133.1 %collective-permute-done.6 = f32[384,1536]{1,0:T(8,128)} collective-permute-done((f32[384,1536]{1,0:T(8,128)}, f32[384,1536]{1,0:T(8,128)}, u32[]{:S(2)}, u32[]{:S(2)}) %collective-permute-start.6) | collective-permute-done | bytes 2359328 | tf_op jit(solution)/shard_map/ppermute | solution.py:13
  477.1 4.7 add_convert_fusion.1
  481.8 45.9 %collective-permute-done.8 = f32[384,1536]{1,0:T(8,128)} collective-permute-done((f32[384,1536]{1,0:T(8,128)}, f32[384,1536]{1,0:T(8,128)}, u32[]{:S(2)}, u32[]{:S(2)}) %collective-permute-start.8) | collective-permute-done | bytes 2359328 | tf_op jit(solution)/shard_map/ppermute | solution.py:13
  527.7 3.9 add_convert_fusion
  (49 shorter events, 30.3 us)
Async XLA Ops:
  0.6 34.7 %copy-start.11 = (s32[384]{0:T(512)S(1)}, s32[384]{0:T(512)}, u32[]{:S(2)}) copy-start(s32[384]{0:T(512)} %param.10) | copy-start | bytes 4612
  0.6 95.4 %copy-start.7 = (bf16[384,1536]{1,0:T(8,128)(2,1)S(1)}, bf16[384,1536]{1,0:T(8,128)(2,1)}, u32[]{:S(2)}) copy-start(bf16[384,1536]{1,0:T(8,128)(2,1)} %param.6) | copy-start | bytes 3538948
  0.7 26.4 %collective-permute-start = (bf16[384,1536]{1,0:T(8,128)(2,1)}, bf16[384,1536]{1,0:T(8,128)(2,1)S(1)}, u32[]{:S(2)}, u32[]{:S(2)}) collective-permute-start(bf16[384,1536]{1,0:T(8,128)(2,1)} %param.8), channel_id=1, source_target_pairs={{0,4},{4,8},{8,12},{12,16},{16,20},{20,24},{24,28},{28,32},{32,36}... | collective-permute-start | bytes 3538952 | tf_op jit(solution)/shard_map/ppermute | solution.py:13
  11.9 91.0 %copy-start.4 = (bf16[384,1536]{0,1:T(8,128)(2,1)}, bf16[384,1536]{0,1:T(8,128)(2,1)S(1)}, u32[]{:S(2)}) copy-start(bf16[384,1536]{0,1:T(8,128)(2,1)S(1)} %copy.34) | copy-start | bytes 3538948
  11.9 85.5 %collective-permute-start.4 = (bf16[384,1536]{0,1:T(8,128)(2,1)S(1)}, bf16[384,1536]{0,1:T(8,128)(2,1)}, u32[]{:S(2)}, u32[]{:S(2)}) collective-permute-start(bf16[384,1536]{0,1:T(8,128)(2,1)S(1)} %copy.34), channel_id=1, source_target_pairs={{0,4},{4,8},{8,12},{12,16},{16,20},{20,24},{24,28},{28,32},{32,36}... | collective-permute-start | bytes 3538952 | tf_op jit(solution)/shard_map/ppermute | solution.py:13
  27.1 75.8 %copy-start.6 = (bf16[384,1536]{1,0:T(8,128)(2,1)}, bf16[384,1536]{1,0:T(8,128)(2,1)S(1)}, u32[]{:S(2)}) copy-start(bf16[384,1536]{1,0:T(8,128)(2,1)S(1)} %collective-permute-done) | copy-start | bytes 3538948
  27.1 75.8 %collective-permute-start.1 = (bf16[384,1536]{1,0:T(8,128)(2,1)S(1)}, bf16[384,1536]{1,0:T(8,128)(2,1)}, u32[]{:S(2)}, u32[]{:S(2)}) collective-permute-start(bf16[384,1536]{1,0:T(8,128)(2,1)S(1)} %collective-permute-done), channel_id=1, source_target_pairs={{0,4},{4,8},{8,12},{12,16},{16,20},{20,24},{24,28},{28,32},{32,36}... | collective-permute-start | bytes 3538952 | tf_op jit(solution)/shard_map/ppermute | solution.py:13
  35.3 51.6 %collective-permute-start.2 = (s32[384]{0:T(512)S(1)}, s32[384]{0:T(512)}, u32[]{:S(2)}, u32[]{:S(2)}) collective-permute-start(s32[384]{0:T(512)S(1)} %copy-done.11), channel_id=1, source_target_pairs={{0,4},{4,8},{8,12},{12,16},{16,20},{20,24},{24,28},{28,32},{32,36}... | collective-permute-start | bytes 4616 | tf_op jit(solution)/shard_map/ppermute | solution.py:13
  87.0 12.4 %collective-permute-start.3 = (s32[384]{0:T(512)}, s32[384]{0:T(512)}, u32[]{:S(2)}, u32[]{:S(2)}) collective-permute-start(s32[384]{0:T(512)} %collective-permute-done.2), channel_id=1, source_target_pairs={{0,4},{4,8},{8,12},{12,16},{16,20},{20,24},{24,28},{28,32},{32,36}... | collective-permute-start | bytes 4616 | tf_op jit(solution)/shard_map/ppermute | solution.py:13
  97.4 24.6 %collective-permute-start.5 = (bf16[384,1536]{0,1:T(8,128)(2,1)}, bf16[384,1536]{0,1:T(8,128)(2,1)}, u32[]{:S(2)}, u32[]{:S(2)}) collective-permute-start(bf16[384,1536]{0,1:T(8,128)(2,1)} %collective-permute-done.4), channel_id=1, source_target_pairs={{0,4},{4,8},{8,12},{12,16},{16,20},{20,24},{24,28},{28,32},{32,36}... | collective-permute-start | bytes 3538952 | tf_op jit(solution)/shard_map/ppermute | solution.py:13
  108.9 15.3 %copy-start.2 = (bf16[384,1536]{0,1:T(8,128)(2,1)S(1)}, bf16[384,1536]{0,1:T(8,128)(2,1)}, u32[]{:S(2)}) copy-start(bf16[384,1536]{0,1:T(8,128)(2,1)} %copy.35) | copy-start | bytes 3538948
  108.9 15.3 %copy-start.5 = (pred[384,1152]{0,1:T(8,128)(4,1)S(1)}, pred[384,1152]{0,1:T(8,128)(4,1)}, u32[]{:S(2)}) copy-start(pred[384,1152]{0,1:T(8,128)(4,1)} %fusion.8) | copy-start | bytes 1327108
  133.4 9.0 %copy-start = (bf16[1152,1536]{0,1:T(8,128)(2,1)S(1)}, bf16[1152,1536]{0,1:T(8,128)(2,1)}, u32[]{:S(2)}) copy-start(bf16[1152,1536]{0,1:T(8,128)(2,1)} %copy.32) | copy-start | bytes 10616836
  142.4 11.9 %copy-start.8 = (f32[12,384]{1,0:T(8,128)}, f32[12,384]{1,0:T(8,128)S(1)}, u32[]{:S(2)}) copy-start(f32[12,384]{1,0:T(8,128)S(1)} %log_add_fusion) | copy-start | bytes 55300
  154.3 3.1 copy-start.10
  175.9 2.4 copy-start.1
  175.9 2.4 copy-start.9
  214.4 129.6 %collective-permute-start.7 = (f32[384,1536]{1,0:T(8,128)}, f32[384,1536]{1,0:T(8,128)}, u32[]{:S(2)}, u32[]{:S(2)}) collective-permute-start(f32[384,1536]{1,0:T(8,128)} %copy.50), channel_id=1, source_target_pairs={{8,0},{12,4},{16,8},{20,12},{24,16},{28,20},{32,24},{36,28},{40,32... | collective-permute-start | bytes 7077896 | tf_op jit(solution)/shard_map/ppermute | solution.py:13
  227.5 249.7 %collective-permute-start.6 = (f32[384,1536]{1,0:T(8,128)}, f32[384,1536]{1,0:T(8,128)}, u32[]{:S(2)}, u32[]{:S(2)}) collective-permute-start(f32[384,1536]{1,0:T(8,128)} %copy.48), channel_id=1, source_target_pairs={{4,0},{8,4},{12,8},{16,12},{20,16},{24,20},{28,24},{32,28},{36,32}... | collective-permute-start | bytes 7077896 | tf_op jit(solution)/shard_map/ppermute | solution.py:13
  258.6 223.2 %collective-permute-start.9 = (f32[384,1536]{1,0:T(8,128)}, f32[384,1536]{1,0:T(8,128)}, u32[]{:S(2)}, u32[]{:S(2)}) collective-permute-start(f32[384,1536]{1,0:T(8,128)} %copy.54), channel_id=1, source_target_pairs={{8,0},{12,4},{16,8},{20,12},{24,16},{28,20},{32,24},{36,28},{40,32... | collective-permute-start | bytes 7077896 | tf_op jit(solution)/shard_map/ppermute | solution.py:13
  263.6 264.1 %collective-permute-start.8 = (f32[384,1536]{1,0:T(8,128)}, f32[384,1536]{1,0:T(8,128)}, u32[]{:S(2)}, u32[]{:S(2)}) collective-permute-start(f32[384,1536]{1,0:T(8,128)} %copy.52), channel_id=1, source_target_pairs={{4,0},{8,4},{12,8},{16,12},{20,16},{24,20},{28,24},{32,28},{36,32}... | collective-permute-start | bytes 7077896 | tf_op jit(solution)/shard_map/ppermute | solution.py:13
  272.9 2.5 copy-start.3
where the time goes:
time: 536 us; the launch traced here: 532 us
  waiting for transfers between devices  320 us (60%)
  matrix products  69.1 us (13%)
  starting transfers between devices  53.9 us (10%)
  local copies, waits for them, and re-layouts  43.6 us (8%)
  other arithmetic  35.8 us (7%)
  blocking collectives  8.69 us (2%)
    ppermute x10, waiting for transfers between devices, from_behind(): lax.ppermute(value, axis, [(source, source + steps) for source in range(i...  320 us
    ppermute x10, starting transfers between devices, from_behind(): lax.ppermute(value, axis, [(source, source + steps) for source in range(i...  53.9 us
    dot_general x1, matrix products, body(): jnp.einsum('qhd,khd->hqk', grad_heads, value_band, preferred_element_type...  16.1 us
    dot_general x1, matrix products, body(): jnp.einsum('hqk,qhd->khd', weights_b, grad_heads, preferred_element_type=...  13.9 us
    slice x3, local copies, waits for them, and re-layouts, body(): key_terms[distance * tok_rows:(distance + 1) * tok_rows]  12.3 us
    slice x3, local copies, waits for them, and re-layouts, body(): value_terms[distance * tok_rows:(distance + 1) * tok_rows]  12.2 us
    dot_general x1, matrix products, body(): jnp.einsum('hqk,khd->qhd', weights_b, value_band, preferred_element_type=...  11.9 us
    dot_general x1, matrix products, body(): jnp.einsum('hqk,qhd->khd', dscore, query_heads, preferred_element_type=jn...  10.8 us
  transfers between devices with their start and end apart: 10, of which 6 were waited for; matrix products, arithmetic and copies ran while one was open for 11% of the time, Pallas kernels for 0%

commit v1 on v0

v1 whole, which is shorter than its diff:
```python
import functools
import math

import jax
import jax.numpy as jnp
from jax import lax
from jax.experimental import pallas as pl
from jax.experimental.pallas import tpu as pltpu
from jax.sharding import PartitionSpec as P

HS = 128
SCALE = HS**-0.5
SCALE2 = SCALE * math.log2(math.e)
HIDDEN = -1e30
CHUNKS = (6, 6)
HANDED = ((0, 3), (3, 6), (6, 12))
STATS = 32
F32 = jnp.float32
BF16 = jnp.bfloat16


def send(value, pairs):
    return lax.ppermute(value, "section", pairs)


def after(value, *earlier):
    return lax.optimization_barrier((value, *earlier))[0]


def dot_nt(a, b):
    return lax.dot_general(a, b, (((1,), (1,)), ((), ())), preferred_element_type=F32)


def dot_nn(a, b):
    return lax.dot_general(a, b, (((1,), (0,)), ((), ())), preferred_element_type=F32)


def as_columns(row):
    return jnp.broadcast_to(row, (128, row.shape[1])).T


def write_bias(bias, key_rows, query_rows, kinds):
    for b, (key_row, query_row, kind) in enumerate(zip(key_rows, query_rows, kinds)):
        n = key_row.shape[1]
        key_doc = jnp.concatenate([as_columns(key_row)] * (n // 128), axis=1)
        visible = key_doc == query_row
        key_pos = lax.broadcasted_iota(jnp.int32, (n, n), 0)
        query_pos = lax.broadcasted_iota(jnp.int32, (n, n), 1)
        if kind == "own":
            visible = visible & (key_pos <= query_pos)
        elif kind == "far":
            visible = visible & (key_pos > query_pos)
        bias[b] = jnp.where(visible, 0.0, HIDDEN)


def choose(core_ref, scratch, for_core0, for_core1):
    @pl.when(core_ref[0] == 0)
    def _():
        scratch[...] = for_core0[...]

    @pl.when(core_ref[0] != 0)
    def _():
        scratch[...] = for_core1[...]


def forward_kernel(
    core_ref, d0, d1, d2, q, k0, kc, kd, k2, v0, vc, vd, v2, cot, gain,
    o, lse, stat, bias, k1, v1, squares, inner,
):
    h = pl.program_id(0)

    @pl.when(h == 0)
    def _():
        rows = [d[0:1, :] for d in (d0, d1, d2)]
        write_bias(bias, rows, [rows[0]] * 3, ("own", "near", "far"))
        squares[...] = jnp.zeros_like(squares)
        inner[...] = jnp.zeros_like(inner)
        lse[...] = jnp.zeros_like(lse)

    choose(core_ref, k1, kd, kc)
    choose(core_ref, v1, vd, vc)
    query = q[...]
    scores = [dot_nt(k[...], query) * SCALE2 + bias[b] for b, k in enumerate((k0, k1, k2))]
    top = functools.reduce(jnp.maximum, [jnp.max(s, axis=0, keepdims=True) for s in scores])
    grown = [jnp.exp2(s - top) for s in scores]
    total = sum(jnp.sum(g, axis=0, keepdims=True) for g in grown)
    over = 1.0 / total
    lse[pl.ds(h, 1), :] = top + jnp.log2(total)
    out = 0.0
    for g, v in zip(grown, (v0, v1, v2)):
        out = out + dot_nn(v[...].T, (g * over).astype(BF16))
    squares[...] += out * out
    out = out.T
    o[...] = out
    inner[...] += cot[...].astype(F32) * gain[...] * out

    @pl.when(h == pl.num_programs(0) - 1)
    def _():
        stat[...] = jnp.zeros_like(stat)
        stat[0:1, :] = jnp.sum(squares[...], axis=0, keepdims=True)
        stat[1:2, :] = jnp.sum(inner[...].T, axis=0, keepdims=True)


def three_parts(value):
    high = value.astype(BF16).astype(F32)
    middle = (value - high).astype(BF16).astype(F32)
    return high, middle, (value - high - middle).astype(BF16).astype(F32)


def norm_kernel(
    features, chunks, docs, parts, lse, o, cot, gain, normed, own_stats, *rest,
):
    pieces, (inv, coef, packed) = rest[:-3], rest[-3:]
    h = pl.program_id(0)

    @pl.when(h == 0)
    def _():
        stat = parts[0:8, :] + parts[8:16, :] + parts[16:24, :] + parts[24:32, :]
        inverse = lax.rsqrt(stat[0:1, :] / features + 1e-05)
        inv[...] = as_columns(inverse)
        coef[...] = as_columns(inverse * inverse * inverse * stat[1:2, :] / features)
        own_stats[...] = jnp.zeros_like(own_stats)
        own_stats[0:16, :] = lse[...]
        own_stats[28:29, :] = docs[0:1, :]

    attended = o[...]
    normed[...] = (attended * inv[...] * gain[...]).astype(BF16)
    out = (inv[...] * (cot[...].astype(F32) * gain[...]) - attended * coef[...]).astype(BF16)
    own_stats[pl.ds(16 + h, 1), :] = jnp.sum((out.astype(F32) * attended).T, axis=0, keepdims=True)
    for piece, (first, end) in zip(pieces, chunks):

        @pl.when((h >= first) & (h < end))
        def _(piece=piece, first=first):
            if first == 0:
                piece[:, pl.ds(pl.multiple_of(h * HS, HS), HS)] = out
            else:
                piece[...] = out

    @pl.when(h == pl.num_programs(0) - 1)
    def _():
        packed[...] = jnp.zeros_like(packed)
        for i, value in enumerate(three_parts(own_stats[...])):
            packed[i * STATS : (i + 1) * STATS, :] = value
        pieces[0][:, chunks[0][1] * HS :] = packed[...].T.astype(BF16)


def own_kernel(
    chunks, core_ref, d0, d1, d2, stats, q, k0, kc, kd, k2, v0, vc, vd, v2, *rest,
):
    pieces, (dq, dk, dv, bias, k1, v1, grad) = rest[:-7], rest[-7:]
    h = pl.program_id(0)

    @pl.when(h == 0)
    def _():
        rows = [d[0:1, :] for d in (d0, d1, d2)]
        write_bias(bias, rows, [rows[0]] * 3, ("own", "near", "far"))

    for piece, (first, end) in zip(pieces, chunks):

        @pl.when((h >= first) & (h < end))
        def _(piece=piece):
            grad[...] = piece[...]

    choose(core_ref, k1, kd, kc)
    choose(core_ref, v1, vd, vc)
    query, out_grad = q[...], grad[...]
    lse = stats[pl.ds(h, 1), :]
    delta = stats[pl.ds(16 + h, 1), :]
    total = 0.0
    for b, (k, v) in enumerate(((k0, v0), (k1, v1), (k2, v2))):
        key = k[...]
        weights = jnp.exp2(dot_nt(key, query) * SCALE2 + bias[b] - lse)
        dscore = (weights * (dot_nt(v[...], out_grad) - delta)).astype(BF16)
        total = total + dot_nn(key.T, dscore)
        if b == 0:
            dk[...] = dot_nn(dscore, query)
            dv[...] = dot_nn(weights.astype(BF16), out_grad)
    dq[...] = (total.T * SCALE).astype(BF16)


def keys_kernel(
    base, aliased, core_ref, docs, pc, pd, p2, k, v, qc, qd, q2, gc, gd, g2, dk0, dv0, *rest,
):
    if aliased:
        rest = rest[2:]
    dk, dv, bias, q1, g1, packed, s1, s2 = rest
    h = pl.program_id(0)

    @pl.when(h == 0)
    def _():
        choose(core_ref, packed, pc, pd)
        for s, p in ((s1, packed), (s2, p2)):
            parts = p[...].astype(F32).T
            s[...] = parts[:STATS] + parts[STATS : 2 * STATS] + parts[2 * STATS : 3 * STATS]
        rows = [s1[28:29, :], s2[28:29, :]]
        write_bias(bias, [docs[0:1, :]] * 2, rows, ("near", "far"))

    choose(core_ref, q1, qc, qd)
    choose(core_ref, g1, gc, gd)
    key, value = k[...], v[...]
    grad_key, grad_value = dk0[...], dv0[...]
    for b, (q, g, stats) in enumerate(((q1, g1, s1), (q2, g2, s2))):
        query, out_grad = q[...], g[...]
        lse = stats[pl.ds(base + h, 1), :]
        delta = stats[pl.ds(16 + base + h, 1), :]
        weights = jnp.exp2(dot_nt(key, query) * SCALE2 + bias[b] - lse)
        dscore = (weights * (dot_nt(value, out_grad) - delta)).astype(BF16)
        grad_key = grad_key + dot_nn(dscore, query)
        grad_value = grad_value + dot_nn(weights.astype(BF16), out_grad)
    dk[...] = (grad_key * SCALE).astype(BF16)
    dv[...] = grad_value.astype(BF16)


def params():
    return dict(
        compiler_params=pltpu.CompilerParams(
            dimension_semantics=("arbitrary",), vmem_limit_bytes=60 * 1024 * 1024
        ),
        cost_estimate=pl.CostEstimate(flops=0, bytes_accessed=0, transcendentals=0),
    )


def body(queries, keys, values, cotangent, doc_ids, gain):
    rows, width = queries.shape
    heads = width // HS
    count = lax.axis_size("section")
    features = width * lax.axis_size("tp")
    section = lax.axis_index("section")
    core = lax.rem(section, 2).astype(jnp.int32).reshape(1)
    ahead = {d: [(s, s + d) for s in range(count) if 0 <= s + d < count] for d in (1, 2, -2)}
    to_core1 = [(s, s + 1) for s in range(0, count, 2)]
    to_core0 = [(s + 1, s) for s in range(0, count, 2)]
    gain = gain.reshape(1, width)

    d0 = jnp.broadcast_to((doc_ids + 1).astype(F32)[None], (8, rows))

    k2 = send(keys, ahead[2])
    v2 = send(values, ahead[2])
    d1 = send(d0, ahead[1])
    d2 = send(d0, ahead[2])
    kc = send(keys, to_core1)
    vc = send(values, to_core1)
    qc = send(queries, to_core0)
    k2, kc, vc, qc, gain = lax.optimization_barrier((k2, kc, vc, qc, gain))
    kd = send(k2, to_core0)
    chunks = [(sum(CHUNKS[:i]), sum(CHUNKS[: i + 1])) for i in range(len(CHUNKS))]
    q_first, q_last = [queries[:, a * HS : b * HS] for a, b in chunks]
    v2, d1, d2, kd, q_first, q_last = lax.optimization_barrier((v2, d1, d2, kd, q_first, q_last))

    q2a = send(q_first, ahead[-2])
    vd = send(v2, to_core0)

    smem = pl.BlockSpec(memory_space=pltpu.SMEM)

    def whole(shape):
        return pl.BlockSpec(shape, lambda h: (0, 0))

    def head(base=0):
        return pl.BlockSpec((rows, HS), lambda h: (0, base + h))

    def part(first, end):
        return pl.BlockSpec((rows, HS), lambda h: (0, jnp.clip(h, first, end - 1) - first))

    def stats_block(at):
        return pl.BlockSpec((rows, HS), lambda h: (0, at))

    def gain_head():
        return pl.BlockSpec((1, HS), lambda h: (0, h))

    tile = pltpu.VMEM((rows, HS), BF16)
    wide = jax.ShapeDtypeStruct((rows, width), F32)
    thin = jax.ShapeDtypeStruct((rows, width), BF16)
    attended, lse, stat = pl.pallas_call(
        forward_kernel,
        grid=(heads,),
        in_specs=[smem] + [whole((8, rows))] * 3 + [head()] * 10 + [gain_head()],
        out_specs=[head(), whole((16, rows)), whole((8, rows))],
        out_shape=[
            wide,
            jax.ShapeDtypeStruct((16, rows), F32),
            jax.ShapeDtypeStruct((8, rows), F32),
        ],
        scratch_shapes=[
            pltpu.VMEM((3, rows, rows), F32),
            tile,
            tile,
            pltpu.VMEM((HS, rows), F32),
            pltpu.VMEM((rows, HS), F32),
        ],
        name="forward",
        **params(),
    )(core, d0, d1, d2, queries, keys, kc, kd, k2, values, vc, vd, v2, cotangent, gain)

    parts = lax.all_gather(after(stat, q2a), "tp", tiled=True)
    q_last = after(q_last, parts)
    q2b = send(q_last, ahead[-2])

    widths = [(b - a) * HS for a, b in chunks]
    widths[0] += HS
    normed, stats, *pieces = pl.pallas_call(
        functools.partial(norm_kernel, features, chunks),
        grid=(heads,),
        in_specs=[whole((8, rows)), whole((32, rows)), whole((16, rows))]
        + [head(), head(), gain_head()],
        out_specs=[head(), whole((STATS, rows)), whole((rows, widths[0]))]
        + [part(*chunk) for chunk in chunks[1:]],
        out_shape=[thin, jax.ShapeDtypeStruct((STATS, rows), F32)]
        + [jax.ShapeDtypeStruct((rows, w), BF16) for w in widths],
        scratch_shapes=[pltpu.VMEM((rows, HS), F32)] * 2 + [pltpu.VMEM((HS, rows), F32)],
        name="norm",
        **params(),
    )(d0, parts, lse, attended, cotangent, gain)

    g2s = [send(piece, ahead[-2]) for piece in pieces]
    gcs = [send(piece, to_core0) for piece in pieces]

    grad_query, dk0, dv0 = pl.pallas_call(
        functools.partial(own_kernel, chunks),
        grid=(heads,),
        in_specs=[smem]
        + [whole((8, rows))] * 3
        + [whole((STATS, rows))]
        + [head()] * 9
        + [part(*chunk) for chunk in chunks],
        out_specs=[head()] * 3,
        out_shape=[thin, wide, wide],
        scratch_shapes=[pltpu.VMEM((3, rows, rows), F32), tile, tile, tile],
        name="own",
        **params(),
    )(core, d0, d1, d2, stats, queries, keys, kc, kd, k2, values, vc, vd, v2, *pieces)

    q2s = [q2a, q2b]
    qds = [send(q, to_core1) for q in lax.optimization_barrier((q2a, q2b, grad_query))[:2]]
    first = after(g2s[0], *qds)
    out = ()
    for a, b in HANDED:
        i = 0 if b <= CHUNKS[0] else 1
        start = a - chunks[i][0]
        if i == 0:
            end = b if b < CHUNKS[0] else b + 1
            gd = send(first[:, a * HS : end * HS], to_core1)
            if b == CHUNKS[0]:
                stats_at = b - a
                pd = gd
        else:
            gd = send(after(g2s[1], *out), to_core1)
        if a == 0:
            waiting = gd
            continue
        steps = [(a, b, gd)]
        if i == 0:
            steps = [(0, a, waiting), (a, b, gd)]
        for a, b, gd in steps:
            start = a - chunks[i][0]
            out = pl.pallas_call(
                functools.partial(keys_kernel, a, len(out) > 0),
                grid=(b - a,),
                in_specs=[smem, whole((8, rows))]
                + [stats_block(CHUNKS[0]), stats_block(stats_at), stats_block(CHUNKS[0])]
                + [head(a)] * 3
                + [head(start)] * 3
                + [head(), head(start)]
                + [head(a)] * 2
                + [pl.BlockSpec(memory_space=pl.ANY)] * len(out),
                out_specs=[head(a)] * 2,
                out_shape=[thin, thin],
                input_output_aliases={15: 0, 16: 1} if out else {},
                scratch_shapes=[pltpu.VMEM((2, rows, rows), F32), tile, tile, tile]
                + [pltpu.VMEM((STATS, rows), F32)] * 2,
                name="keys",
                **params(),
            )(
                core, d0, gcs[0], pd, g2s[0], keys, values, qc, qds[i], q2s[i],
                gcs[i], gd, g2s[i], dk0, dv0, *out,
            )
    return normed, grad_query, out[0], out[1]


def solution(mesh):
    split = P("section", "tp")
    return jax.shard_map(
        body,
        mesh=mesh,
        in_specs=(split, split, split, split, P("section"), P("tp")),
        out_specs=(split, split, split, split),
        check_vma=False,
    )
```

time: 536 us -> 277 us (0.52)
  waiting for transfers between devices: 320 us -> 59.4 us
  starting transfers between devices: 53.9 us -> 126 us
  matrix products: 69.1 us -> 0 us
  Pallas kernels: 0 us -> 69.1 us
  other arithmetic: 35.8 us -> 0.69 us
  local copies, waits for them, and re-layouts: 43.6 us -> 8.6 us
    ppermute x10 -> x20, waiting for transfers between devices: 320 us -> 59.4 us  [send(): return lax.ppermute(value, 'section', pairs)]
    ppermute x10 -> x20, starting transfers between devices: 53.9 us -> 126 us  [send(): return lax.ppermute(value, 'section', pairs)]
    pallas_call x0 -> x6, Pallas kernels: none -> 69.1 us  [the longest x3 20.5 us: body(): pl.pallas_call(functools.partial(keys_kernel, a, len(out) > 0), grid=(b -...]
    dot_general x6 -> x0, matrix products: 69.1 us -> none  [the longest x1 16.1 us: body(): jnp.einsum('qhd,khd->hqk', grad_heads, value_band, preferred_element_type...]
    slice x8 -> x3, local copies, waits for them, and re-layouts: 28.6 us -> 2.39 us  [the longest x1 2.33 us: body(): q_first, q_last = [queries[:, a * HS:b * HS] for a, b in chunks]]
    reduce_sum x3 -> x0, other arithmetic: 13.7 us -> none  [the longest x1 8.96 us: body(): jnp.sum(jnp.exp(scores - row_max), axis=-1, keepdims=True)]
    convert_element_type x3 -> x1, other arithmetic: 13 us -> 0.69 us  [body(): d0 = jnp.broadcast_to((doc_ids + 1).astype(F32)[None], (8, rows))]
    all_gather x0 -> x1, blocking collectives: none -> 11.1 us  [body(): parts = lax.all_gather(after(stat, q2a), 'tp', tiled=True)]
  transfers between devices with their start and end apart: 10 -> 20, of which waited for: 6 -> 6; matrix products, arithmetic and copies ran while one was open for 11% -> 2% of each run, Pallas kernels for 0% -> 22%
where the time goes in v1:
time: 277 us; the launch traced here: 276 us
  starting transfers between devices  126 us (45%)
  Pallas kernels  69.1 us (25%)
  waiting for transfers between devices  59.4 us (21%)
  blocking collectives  11.1 us (4%)
  local copies, waits for them, and re-layouts  8.6 us (3%)
    ppermute x20, starting transfers between devices, send(): return lax.ppermute(value, 'section', pairs)  126 us
    ppermute x20, waiting for transfers between devices, send(): return lax.ppermute(value, 'section', pairs)  59.4 us
    pallas_call x3, Pallas kernels, body(): pl.pallas_call(functools.partial(keys_kernel, a, len(out) > 0), grid=(b -...  20.5 us
    pallas_call x1, Pallas kernels, body(): pl.pallas_call(functools.partial(own_kernel, chunks), grid=(heads,), in_s...  20.3 us
    pallas_call x1, Pallas kernels, body(): pl.pallas_call(forward_kernel, grid=(heads,), in_specs=[smem] + [whole((8...  19 us
    all_gather x1, blocking collectives, body(): parts = lax.all_gather(after(stat, q2a), 'tp', tiled=True)  11.1 us
    pallas_call x1, Pallas kernels, body(): pl.pallas_call(functools.partial(norm_kernel, features, chunks), grid=(he...  9.28 us
  transfers between devices with their start and end apart: 20, of which 6 were waited for; matrix products, arithmetic and copies ran while one was open for 2% of the time, Pallas kernels for 22%

profile of v1, /device:TPU:5, one launch (start us, length us, event | category | flops | bytes accessed | tf_op | source)
XLA Modules:
  0.0 275.5 jit_solution(12522664426403912708)
XLA Ops:
  0.6 8.8 %collective-permute-start.3 = (bf16[384,1536]{1,0:T(8,128)(2,1)}, bf16[384,1536]{1,0:T(8,128)(2,1)S(1)}, u32[]{:S(2)}, u32[]{:S(2)}) collective-permute-start(bf16[384,1536]{1,0:T(8,128)(2,1)} %k.5), channel_id=1, source_target_pairs={{0,8},{4,12},{8,16},{12,20},{16,24},{20,28},{24,32},{28,36},{32,40... | collective-permute-start | bytes 3538952 | tf_op jit(solution)/shard_map/ppermute | solution.py:23
  9.5 1.3 collective-permute-start.4
  12.1 3.3 %collective-permute-start.6 = (bf16[384,1536]{1,0:T(8,128)(2,1)}, bf16[384,1536]{1,0:T(8,128)(2,1)S(1)}, u32[]{:S(2)}, u32[]{:S(2)}) collective-permute-start(bf16[384,1536]{1,0:T(8,128)(2,1)} %q.3), channel_id=1, source_target_pairs={{4,0},{12,8},{20,16},{28,24},{36,32},{44,40},{52,48},{60,56},{68,6... | collective-permute-start | bytes 3538952 | tf_op jit(solution)/shard_map/ppermute | solution.py:23
  15.3 1.9 collective-permute-start
  17.3 1.3 reshape.16.gain
  18.5 26.7 %collective-permute-done.3.k2 = bf16[384,1536]{1,0:T(8,128)(2,1)S(1)} collective-permute-done((bf16[384,1536]{1,0:T(8,128)(2,1)}, bf16[384,1536]{1,0:T(8,128)(2,1)S(1)}, u32[]{:S(2)}, u32[]{:S(2)}) %collective-permute-start.3) | collective-permute-done | bytes 1179680 | tf_op jit(solution)/shard_map/ppermute | solution.py:23
  46.3 4.2 %collective-permute-start.7 = (bf16[384,1536]{1,0:T(8,128)(2,1)S(1)}, bf16[384,1536]{1,0:T(8,128)(2,1)S(1)}, u32[]{:S(2)}, u32[]{:S(2)}) collective-permute-start(bf16[384,1536]{1,0:T(8,128)(2,1)S(1)} %collective-permute-done.3.k2), channel_id=1, source_target_pairs={{4,0},{12,8},{20,16},{28,24},{36,32},{44,40},{52,48},{60,56},{68,6... | collective-permute-start | bytes 3538952 | tf_op jit(solution)/shard_map/ppermute | solution.py:23
  51.2 4.1 %collective-permute-start.1 = (f32[8,384]{1,0:T(8,128)S(1)}, f32[8,384]{1,0:T(8,128)S(1)}, u32[]{:S(2)}, u32[]{:S(2)}) collective-permute-start(f32[8,384]{1,0:T(8,128)S(1)} %broadcast_in_dim.2.d0.docs), channel_id=1, source_target_pairs={{0,4},{4,8},{8,12},{12,16},{16,20},{20,24},{24,28},{28,32},{32,36}... | collective-permute-start | bytes 36872 | tf_op jit(solution)/shard_map/ppermute | solution.py:23
  55.3 2.7 collective-permute-start.2
  58.0 2.3 fusion
  60.3 18.2 %collective-permute-done.1.d1 = f32[8,384]{1,0:T(8,128)S(1)} collective-permute-done((f32[8,384]{1,0:T(8,128)S(1)}, f32[8,384]{1,0:T(8,128)S(1)}, u32[]{:S(2)}, u32[]{:S(2)}) %collective-permute-start.1) | collective-permute-done | bytes 12320 | tf_op jit(solution)/shard_map/ppermute | solution.py:23
  78.5 5.4 %collective-permute-done.2.d2 = f32[8,384]{1,0:T(8,128)S(1)} collective-permute-done((f32[8,384]{1,0:T(8,128)S(1)}, f32[8,384]{1,0:T(8,128)S(1)}, u32[]{:S(2)}, u32[]{:S(2)}) %collective-permute-start.2) | collective-permute-done | bytes 12320 | tf_op jit(solution)/shard_map/ppermute | solution.py:23
  84.9 30.9 %collective-permute-start.8 = (bf16[384,1536]{1,0:T(8,128)(2,1)}, bf16[384,1536]{1,0:T(8,128)(2,1)S(1)}, u32[]{:S(2)}, u32[]{:S(2)}) collective-permute-start(bf16[384,1536]{1,0:T(8,128)(2,1)} %collective-permute-done.v2), channel_id=1, source_target_pairs={{4,0},{12,8},{20,16},{28,24},{36,32},{44,40},{52,48},{60,56},{68,6... | collective-permute-start | bytes 3538952 | tf_op jit(solution)/shard_map/ppermute | solution.py:23
  115.8 10.5 %collective-permute-start.9 = (bf16[384,768]{1,0:T(8,128)(2,1)}, bf16[384,768]{1,0:T(8,128)(2,1)S(1)}, u32[]{:S(2)}, u32[]{:S(2)}) collective-permute-start(bf16[384,768]{1,0:T(8,128)(2,1)} %get-tuple-element.46), channel_id=1, source_target_pairs={{8,0},{12,4},{16,8},{20,12},{24,16},{28,20},{32,24},{36,28},{40,32... | collective-permute-start | bytes 1769480 | tf_op jit(solution)/shard_map/ppermute | solution.py:23
  127.4 19.0 %forward.1 = (f32[384,1536]{1,0:T(8,128)}, f32[16,384]{1,0:T(8,128)}, f32[8,384]{1,0:T(8,128)}) custom-call(s32[1]{0:T(128)} %bitcast.core_ref, f32[8,384]{1,0:T(8,128)} %copy-done.12, f32[8,384]{1,0:T(8,128)} %copy-done.17, f32[8,384]{1,0:T(8,128)} %copy-done.18, bf16[384,1536]{1,0:T(8,128)(2,1)} %q.3, bf16[384,1536]{1,0:T(8,128)(2,1)} %k.5, ...), custom_call_target="tpu_custom_call" | custom-call | tf_op jit(solution)/shard_map/forward/pallas_call | solution.py:273
  146.4 5.8 %collective-permute-done.9.q2 = bf16[384,768]{1,0:T(8,128)(2,1)S(1)} collective-permute-done((bf16[384,768]{1,0:T(8,128)(2,1)}, bf16[384,768]{1,0:T(8,128)(2,1)S(1)}, u32[]{:S(2)}, u32[]{:S(2)}) %collective-permute-start.9) | collective-permute-done | bytes 589856 | tf_op jit(solution)/shard_map/ppermute | solution.py:23
  152.2 11.1 %all_gather.3.parts = f32[32,384]{1,0:T(8,128)} all-gather(f32[8,384]{1,0:T(8,128)} %get-tuple-element.47), channel_id=1, replica_groups=mesh['section'=64,'tp'=4] {'tp'}, dimensions={0}, use_global_device_ids=true | all-gather | bytes 61440 | tf_op jit(solution)/shard_map/all_gather | solution.py:294
  163.3 10.7 %collective-permute-start.12 = (bf16[384,768]{1,0:T(8,128)(2,1)S(1)}, bf16[384,768]{1,0:T(8,128)(2,1)}, u32[]{:S(2)}, u32[]{:S(2)}) collective-permute-start(bf16[384,768]{1,0:T(8,128)(2,1)S(1)} %copy-done.15), channel_id=1, source_target_pairs={{8,0},{12,4},{16,8},{20,12},{24,16},{28,20},{32,24},{36,28},{40,32... | collective-permute-start | bytes 1769480 | tf_op jit(solution)/shard_map/ppermute | solution.py:23
  174.1 9.3 %norm.1 = (bf16[384,1536]{1,0:T(8,128)(2,1)}, f32[32,384]{1,0:T(8,128)}, bf16[384,896]{1,0:T(8,128)(2,1)}, bf16[384,768]{1,0:T(8,128)(2,1)}) custom-call(f32[8,384]{1,0:T(8,128)} %copy-done.12, f32[32,384]{1,0:T(8,128)} %all_gather.3.parts, f32[16,384]{1,0:T(8,128)} %get-tuple-element.48.lse, f32[384,1536]{1,0:T(8,128)} %get-tuple-element.49.o, ...), custom_call_target="tpu_custom_call" | custom-call | tf_op jit(solution)/shard_map/norm/pallas_call | solution.py:300
  183.3 1.9 collective-permute-start.11
  185.3 20.3 %own.1 = (bf16[384,1536]{1,0:T(8,128)(2,1)}, f32[384,1536]{1,0:T(8,128)}, f32[384,1536]{1,0:T(8,128)}) custom-call(s32[1]{0:T(128)} %bitcast.core_ref, f32[8,384]{1,0:T(8,128)} %copy-done.12, f32[8,384]{1,0:T(8,128)} %copy-done.17, f32[8,384]{1,0:T(8,128)} %copy-done.18, f32[32,384]{1,0:T(8,128)} %get-tuple-element.51.stats, bf16[384,1536]{1,0:T(8,128)(2,1)} %q.3, ...), custom_call_target="tpu_custom_call" | custom-call | tf_op jit(solution)/shard_map/own/pallas_call | solution.py:317
  205.6 1.3 collective-permute-start.13
  206.9 1.3 collective-permute-start.14
  208.2 6.8 %collective-permute-start.10 = (bf16[384,896]{1,0:T(8,128)(2,1)S(1)}, bf16[384,896]{1,0:T(8,128)(2,1)S(1)}, u32[]{:S(2)}, u32[]{:S(2)}) collective-permute-start(bf16[384,896]{1,0:T(8,128)(2,1)S(1)} %copy-done.11), channel_id=1, source_target_pairs={{4,0},{12,8},{20,16},{28,24},{36,32},{44,40},{52,48},{60,56},{68,6... | collective-permute-start | bytes 2064392 | tf_op jit(solution)/shard_map/ppermute | solution.py:23
  215.0 15.2 %collective-permute-start.17 = (bf16[384,768]{1,0:T(8,128)(2,1)}, bf16[384,768]{1,0:T(8,128)(2,1)}, u32[]{:S(2)}, u32[]{:S(2)}) collective-permute-start(bf16[384,768]{1,0:T(8,128)(2,1)} %get-tuple-element.53.rest_1_), channel_id=1, source_target_pairs={{8,0},{12,4},{16,8},{20,12},{24,16},{28,20},{32,24},{36,28},{40,32... | collective-permute-start | bytes 1769480 | tf_op jit(solution)/shard_map/ppermute | solution.py:23
  230.8 1.3 collective-permute-start.15
  233.4 15.5 %collective-permute-start.16 = (bf16[384,768]{1,0:T(8,128)(2,1)}, bf16[384,768]{1,0:T(8,128)(2,1)S(1)}, u32[]{:S(2)}, u32[]{:S(2)}) collective-permute-start(bf16[384,768]{1,0:T(8,128)(2,1)} %get-tuple-element.53.rest_1_), channel_id=1, source_target_pairs={{4,0},{12,8},{20,16},{28,24},{36,32},{44,40},{52,48},{60,56},{68,6... | collective-permute-start | bytes 1769480 | tf_op jit(solution)/shard_map/ppermute | solution.py:23
  250.1 5.7 %keys.3 = (bf16[384,1536]{1,0:T(8,128)(2,1)}, bf16[384,1536]{1,0:T(8,128)(2,1)}) custom-call(s32[1]{0:T(128)} %bitcast.core_ref, f32[8,384]{1,0:T(8,128)} %copy-done.12, bf16[384,896]{1,0:T(8,128)(2,1)} %copy-done.1, bf16[384,512]{1,0:T(8,128)(2,1)} %copy-done.3, bf16[384,896]{1,0:T(8,128)(2,1)} %copy-done, bf16[384,1536]{1,0:T(8,128)(2,1)} %k.5, ...), custom_call_target="tpu_custom_call" | custom-call | tf_op jit(solution)/shard_map/keys/pallas_call | solution.py:355
  255.8 5.8 %keys.4 = (bf16[384,1536]{1,0:T(8,128)(2,1)}, bf16[384,1536]{1,0:T(8,128)(2,1)}) custom-call(s32[1]{0:T(128)} %bitcast.core_ref, f32[8,384]{1,0:T(8,128)} %copy-done.12, bf16[384,896]{1,0:T(8,128)(2,1)} %copy-done.1, bf16[384,512]{1,0:T(8,128)(2,1)} %copy-done.3, bf16[384,896]{1,0:T(8,128)(2,1)} %copy-done, ...), custom_call_target="tpu_custom_call", output_to_operand_aliasing={{0}: (15, {}), {1}: (16, {})} | custom-call | tf_op jit(solution)/shard_map/keys/pallas_call | solution.py:355
  261.6 1.3 collective-permute-start.19
  262.9 2.8 %collective-permute-done.19.gd = bf16[384,768]{1,0:T(8,128)(2,1)S(1)} collective-permute-done((bf16[384,768]{1,0:T(8,128)(2,1)}, bf16[384,768]{1,0:T(8,128)(2,1)S(1)}, u32[]{:S(2)}, u32[]{:S(2)}) %collective-permute-start.19) | collective-permute-done | bytes 589856 | tf_op jit(solution)/shard_map/ppermute | solution.py:23
  266.5 9.1 %keys.5 = (bf16[384,1536]{1,0:T(8,128)(2,1)}, bf16[384,1536]{1,0:T(8,128)(2,1)}) custom-call(s32[1]{0:T(128)} %bitcast.core_ref, f32[8,384]{1,0:T(8,128)} %copy-done.12, bf16[384,896]{1,0:T(8,128)(2,1)} %copy-done.1, bf16[384,512]{1,0:T(8,128)(2,1)} %copy-done.3, bf16[384,896]{1,0:T(8,128)(2,1)} %copy-done, ...), custom_call_target="tpu_custom_call", output_to_operand_aliasing={{0}: (15, {}), {1}: (16, {})} | custom-call | tf_op jit(solution)/shard_map/keys/pallas_call | solution.py:355
  (59 shorter events, 8.8 us)
Async XLA Ops:
  0.6 44.6 %collective-permute-start.3 = (bf16[384,1536]{1,0:T(8,128)(2,1)}, bf16[384,1536]{1,0:T(8,128)(2,1)S(1)}, u32[]{:S(2)}, u32[]{:S(2)}) collective-permute-start(bf16[384,1536]{1,0:T(8,128)(2,1)} %k.5), channel_id=1, source_target_pairs={{0,8},{4,12},{8,16},{12,20},{16,24},{20,28},{24,32},{28,36},{32,40... | collective-permute-start | bytes 3538952 | tf_op jit(solution)/shard_map/ppermute | solution.py:23
  9.5 35.8 %collective-permute-start.4 = (bf16[384,1536]{1,0:T(8,128)(2,1)}, bf16[384,1536]{1,0:T(8,128)(2,1)S(1)}, u32[]{:S(2)}, u32[]{:S(2)}) collective-permute-start(bf16[384,1536]{1,0:T(8,128)(2,1)} %k.5), channel_id=1, source_target_pairs={{0,4},{8,12},{16,20},{24,28},{32,36},{40,44},{48,52},{56,60},{64,6... | collective-permute-start | bytes 3538952 | tf_op jit(solution)/shard_map/ppermute | solution.py:23
  10.8 34.5 %collective-permute-start.5 = (bf16[384,1536]{1,0:T(8,128)(2,1)}, bf16[384,1536]{1,0:T(8,128)(2,1)S(1)}, u32[]{:S(2)}, u32[]{:S(2)}) collective-permute-start(bf16[384,1536]{1,0:T(8,128)(2,1)} %v.5), channel_id=1, source_target_pairs={{0,4},{8,12},{16,20},{24,28},{32,36},{40,44},{48,52},{56,60},{64,6... | collective-permute-start | bytes 3538952 | tf_op jit(solution)/shard_map/ppermute | solution.py:23
  12.1 33.2 %collective-permute-start.6 = (bf16[384,1536]{1,0:T(8,128)(2,1)}, bf16[384,1536]{1,0:T(8,128)(2,1)S(1)}, u32[]{:S(2)}, u32[]{:S(2)}) collective-permute-start(bf16[384,1536]{1,0:T(8,128)(2,1)} %q.3), channel_id=1, source_target_pairs={{4,0},{12,8},{20,16},{28,24},{36,32},{44,40},{52,48},{60,56},{68,6... | collective-permute-start | bytes 3538952 | tf_op jit(solution)/shard_map/ppermute | solution.py:23
  15.3 68.6 %collective-permute-start = (bf16[384,1536]{1,0:T(8,128)(2,1)}, bf16[384,1536]{1,0:T(8,128)(2,1)}, u32[]{:S(2)}, u32[]{:S(2)}) collective-permute-start(bf16[384,1536]{1,0:T(8,128)(2,1)} %v.5), channel_id=1, source_target_pairs={{0,8},{4,12},{8,16},{12,20},{16,24},{20,28},{24,32},{28,36},{32,40... | collective-permute-start | bytes 3538952 | tf_op jit(solution)/shard_map/ppermute | solution.py:23
  45.2 15.1 %copy-start.4 = (bf16[384,1536]{1,0:T(8,128)(2,1)}, bf16[384,1536]{1,0:T(8,128)(2,1)S(1)}, u32[]{:S(2)}) copy-start(bf16[384,1536]{1,0:T(8,128)(2,1)S(1)} %collective-permute-done.3.k2) | copy-start | bytes 3538948
  45.2 5.2 %copy-start.6 = (bf16[384,1536]{1,0:T(8,128)(2,1)}, bf16[384,1536]{1,0:T(8,128)(2,1)S(1)}, u32[]{:S(2)}) copy-start(bf16[384,1536]{1,0:T(8,128)(2,1)S(1)} %collective-permute-done.5.vc) | copy-start | bytes 3538948
  46.3 14.1 %copy-start.2 = (bf16[384,1536]{1,0:T(8,128)(2,1)}, bf16[384,1536]{1,0:T(8,128)(2,1)S(1)}, u32[]{:S(2)}) copy-start(bf16[384,1536]{1,0:T(8,128)(2,1)S(1)} %collective-permute-done.6.qc) | copy-start | bytes 3538948
  46.3 37.6 %collective-permute-start.7 = (bf16[384,1536]{1,0:T(8,128)(2,1)S(1)}, bf16[384,1536]{1,0:T(8,128)(2,1)S(1)}, u32[]{:S(2)}, u32[]{:S(2)}) collective-permute-start(bf16[384,1536]{1,0:T(8,128)(2,1)S(1)} %collective-permute-done.3.k2), channel_id=1, source_target_pairs={{4,0},{12,8},{20,16},{28,24},{36,32},{44,40},{52,48},{60,56},{68,6... | collective-permute-start | bytes 3538952 | tf_op jit(solution)/shard_map/ppermute | solution.py:23
  51.2 9.2 %copy-start.12 = (f32[8,384]{1,0:T(8,128)}, f32[8,384]{1,0:T(8,128)S(1)}, u32[]{:S(2)}) copy-start(f32[8,384]{1,0:T(8,128)S(1)} %broadcast_in_dim.2.d0.docs) | copy-start | bytes 36868
  51.2 27.3 %collective-permute-start.1 = (f32[8,384]{1,0:T(8,128)S(1)}, f32[8,384]{1,0:T(8,128)S(1)}, u32[]{:S(2)}, u32[]{:S(2)}) collective-permute-start(f32[8,384]{1,0:T(8,128)S(1)} %broadcast_in_dim.2.d0.docs), channel_id=1, source_target_pairs={{0,4},{4,8},{8,12},{12,16},{16,20},{20,24},{24,28},{28,32},{32,36}... | collective-permute-start | bytes 36872 | tf_op jit(solution)/shard_map/ppermute | solution.py:23
  55.3 28.6 %collective-permute-start.2 = (f32[8,384]{1,0:T(8,128)S(1)}, f32[8,384]{1,0:T(8,128)S(1)}, u32[]{:S(2)}, u32[]{:S(2)}) collective-permute-start(f32[8,384]{1,0:T(8,128)S(1)} %broadcast_in_dim.2.d0.docs), channel_id=1, source_target_pairs={{0,8},{4,12},{8,16},{12,20},{16,24},{20,28},{24,32},{28,36},{32,40... | collective-permute-start | bytes 36872 | tf_op jit(solution)/shard_map/ppermute | solution.py:23
  78.5 47.9 %copy-start.17 = (f32[8,384]{1,0:T(8,128)}, f32[8,384]{1,0:T(8,128)S(1)}, u32[]{:S(2)}) copy-start(f32[8,384]{1,0:T(8,128)S(1)} %collective-permute-done.1.d1) | copy-start | bytes 36868
  83.9 42.5 %copy-start.18 = (f32[8,384]{1,0:T(8,128)}, f32[8,384]{1,0:T(8,128)S(1)}, u32[]{:S(2)}) copy-start(f32[8,384]{1,0:T(8,128)S(1)} %collective-permute-done.2.d2) | copy-start | bytes 36868
  84.9 41.5 %collective-permute-start.8 = (bf16[384,1536]{1,0:T(8,128)(2,1)}, bf16[384,1536]{1,0:T(8,128)(2,1)S(1)}, u32[]{:S(2)}, u32[]{:S(2)}) collective-permute-start(bf16[384,1536]{1,0:T(8,128)(2,1)} %collective-permute-done.v2), channel_id=1, source_target_pairs={{4,0},{12,8},{20,16},{28,24},{36,32},{44,40},{52,48},{60,56},{68,6... | collective-permute-start | bytes 3538952 | tf_op jit(solution)/shard_map/ppermute | solution.py:23
  115.8 36.4 %collective-permute-start.9 = (bf16[384,768]{1,0:T(8,128)(2,1)}, bf16[384,768]{1,0:T(8,128)(2,1)S(1)}, u32[]{:S(2)}, u32[]{:S(2)}) collective-permute-start(bf16[384,768]{1,0:T(8,128)(2,1)} %get-tuple-element.46), channel_id=1, source_target_pairs={{8,0},{12,4},{16,8},{20,12},{24,16},{28,20},{32,24},{36,28},{40,32... | collective-permute-start | bytes 1769480 | tf_op jit(solution)/shard_map/ppermute | solution.py:23
  127.4 35.9 %copy-start.15 = (bf16[384,768]{1,0:T(8,128)(2,1)S(1)}, bf16[384,768]{1,0:T(8,128)(2,1)}, u32[]{:S(2)}) copy-start(bf16[384,768]{1,0:T(8,128)(2,1)} %get-tuple-element.56) | copy-start | bytes 1769476
  152.2 53.4 %copy-start.9 = (bf16[384,768]{1,0:T(8,128)(2,1)}, bf16[384,768]{1,0:T(8,128)(2,1)S(1)}, u32[]{:S(2)}) copy-start(bf16[384,768]{1,0:T(8,128)(2,1)S(1)} %collective-permute-done.9.q2) | copy-start | bytes 1769476
  163.3 42.3 %collective-permute-start.12 = (bf16[384,768]{1,0:T(8,128)(2,1)S(1)}, bf16[384,768]{1,0:T(8,128)(2,1)}, u32[]{:S(2)}, u32[]{:S(2)}) collective-permute-start(bf16[384,768]{1,0:T(8,128)(2,1)S(1)} %copy-done.15), channel_id=1, source_target_pairs={{8,0},{12,4},{16,8},{20,12},{24,16},{28,20},{32,24},{36,28},{40,32... | collective-permute-start | bytes 1769480 | tf_op jit(solution)/shard_map/ppermute | solution.py:23
  183.3 47.4 %collective-permute-start.11 = (bf16[384,896]{1,0:T(8,128)(2,1)}, bf16[384,896]{1,0:T(8,128)(2,1)S(1)}, u32[]{:S(2)}, u32[]{:S(2)}) collective-permute-start(bf16[384,896]{1,0:T(8,128)(2,1)} %get-tuple-element.52.rest_0_), channel_id=1, source_target_pairs={{8,0},{12,4},{16,8},{20,12},{24,16},{28,20},{32,24},{36,28},{40,32... | collective-permute-start | bytes 2064392 | tf_op jit(solution)/shard_map/ppermute | solution.py:23
  185.3 23.0 %copy-start.11 = (bf16[384,896]{1,0:T(8,128)(2,1)S(1)}, bf16[384,896]{1,0:T(8,128)(2,1)}, u32[]{:S(2)}) copy-start(bf16[384,896]{1,0:T(8,128)(2,1)} %get-tuple-element.52.rest_0_) | copy-start | bytes 2064388
  205.6 25.1 %collective-permute-start.13 = (bf16[384,768]{1,0:T(8,128)(2,1)S(1)}, bf16[384,768]{1,0:T(8,128)(2,1)S(1)}, u32[]{:S(2)}, u32[]{:S(2)}) collective-permute-start(bf16[384,768]{1,0:T(8,128)(2,1)S(1)} %collective-permute-done.9.q2), channel_id=1, source_target_pairs={{0,4},{8,12},{16,20},{24,28},{32,36},{40,44},{48,52},{56,60},{64,6... | collective-permute-start | bytes 1769480 | tf_op jit(solution)/shard_map/ppermute | solution.py:23
  206.9 23.8 %collective-permute-start.14 = (bf16[384,768]{1,0:T(8,128)(2,1)}, bf16[384,768]{1,0:T(8,128)(2,1)}, u32[]{:S(2)}, u32[]{:S(2)}) collective-permute-start(bf16[384,768]{1,0:T(8,128)(2,1)} %collective-permute-done.12.q2), channel_id=1, source_target_pairs={{0,4},{8,12},{16,20},{24,28},{32,36},{40,44},{48,52},{56,60},{64,6... | collective-permute-start | bytes 1769480 | tf_op jit(solution)/shard_map/ppermute | solution.py:23
  208.2 40.7 %collective-permute-start.10 = (bf16[384,896]{1,0:T(8,128)(2,1)S(1)}, bf16[384,896]{1,0:T(8,128)(2,1)S(1)}, u32[]{:S(2)}, u32[]{:S(2)}) collective-permute-start(bf16[384,896]{1,0:T(8,128)(2,1)S(1)} %copy-done.11), channel_id=1, source_target_pairs={{4,0},{12,8},{20,16},{28,24},{36,32},{44,40},{52,48},{60,56},{68,6... | collective-permute-start | bytes 2064392 | tf_op jit(solution)/shard_map/ppermute | solution.py:23
  215.0 46.5 %collective-permute-start.17 = (bf16[384,768]{1,0:T(8,128)(2,1)}, bf16[384,768]{1,0:T(8,128)(2,1)}, u32[]{:S(2)}, u32[]{:S(2)}) collective-permute-start(bf16[384,768]{1,0:T(8,128)(2,1)} %get-tuple-element.53.rest_1_), channel_id=1, source_target_pairs={{8,0},{12,4},{16,8},{20,12},{24,16},{28,20},{32,24},{36,28},{40,32... | collective-permute-start | bytes 1769480 | tf_op jit(solution)/shard_map/ppermute | solution.py:23
  230.7 18.3 %copy-start = (bf16[384,896]{1,0:T(8,128)(2,1)}, bf16[384,896]{1,0:T(8,128)(2,1)S(1)}, u32[]{:S(2)}) copy-start(bf16[384,896]{1,0:T(8,128)(2,1)S(1)} %collective-permute-done.11.p2.g2) | copy-start | bytes 2064388
  230.7 18.3 %copy-start.10 = (bf16[384,768]{1,0:T(8,128)(2,1)}, bf16[384,768]{1,0:T(8,128)(2,1)S(1)}, u32[]{:S(2)}) copy-start(bf16[384,768]{1,0:T(8,128)(2,1)S(1)} %collective-permute-done.13.qd) | copy-start | bytes 1769476
  230.8 18.2 %collective-permute-start.15 = (bf16[384,512]{1,0:T(8,128)(2,1)S(1)}, bf16[384,512]{1,0:T(8,128)(2,1)S(1)}, u32[]{:S(2)}, u32[]{:S(2)}) collective-permute-start(bf16[384,512]{1,0:T(8,128)(2,1)S(1)} %slice.14), channel_id=1, source_target_pairs={{0,4},{8,12},{16,20},{24,28},{32,36},{40,44},{48,52},{56,60},{64,6... | collective-permute-start | bytes 1179656 | tf_op jit(solution)/shard_map/ppermute | solution.py:23
  232.1 16.8 %collective-permute-start.18 = (bf16[384,384]{1,0:T(8,128)(2,1)S(1)}, bf16[384,384]{1,0:T(8,128)(2,1)S(1)}, u32[]{:S(2)}, u32[]{:S(2)}) collective-permute-start(bf16[384,384]{1,0:T(8,128)(2,1)S(1)} %slice.15), channel_id=1, source_target_pairs={{0,4},{8,12},{16,20},{24,28},{32,36},{40,44},{48,52},{56,60},{64,6... | collective-permute-start | bytes 884744 | tf_op jit(solution)/shard_map/ppermute | solution.py:23
  233.4 29.4 %collective-permute-start.16 = (bf16[384,768]{1,0:T(8,128)(2,1)}, bf16[384,768]{1,0:T(8,128)(2,1)S(1)}, u32[]{:S(2)}, u32[]{:S(2)}) collective-permute-start(bf16[384,768]{1,0:T(8,128)(2,1)} %get-tuple-element.53.rest_1_), channel_id=1, source_target_pairs={{4,0},{12,8},{20,16},{28,24},{36,32},{44,40},{52,48},{60,56},{68,6... | collective-permute-start | bytes 1769480 | tf_op jit(solution)/shard_map/ppermute | solution.py:23
  261.6 4.1 %collective-permute-start.19 = (bf16[384,768]{1,0:T(8,128)(2,1)}, bf16[384,768]{1,0:T(8,128)(2,1)S(1)}, u32[]{:S(2)}, u32[]{:S(2)}) collective-permute-start(bf16[384,768]{1,0:T(8,128)(2,1)} %collective-permute-done.17.g2), channel_id=1, source_target_pairs={{0,4},{8,12},{16,20},{24,28},{32,36},{40,44},{48,52},{56,60},{64,6... | collective-permute-start | bytes 1769480 | tf_op jit(solution)/shard_map/ppermute | solution.py:23
  262.9 2.8 %copy-start.13 = (bf16[384,768]{1,0:T(8,128)(2,1)}, bf16[384,768]{1,0:T(8,128)(2,1)S(1)}, u32[]{:S(2)}) copy-start(bf16[384,768]{1,0:T(8,128)(2,1)S(1)} %collective-permute-done.16.gc) | copy-start | bytes 1769476
  (7 other events, 6.7 us)

commit v2 on v1

--- a/solution.py
+++ b/solution.py
@@ -13,7 +13,8 @@
 SCALE2 = SCALE * math.log2(math.e)
 HIDDEN = -1e30
 CHUNKS = (6, 6)
-HANDED = ((0, 3), (3, 6), (6, 12))
+HANDED = ((0, 2), (2, 4), (4, 6))
+QUERIES = 5
 STATS = 32
 F32 = jnp.float32
 BF16 = jnp.bfloat16
@@ -63,6 +64,14 @@
         scratch[...] = for_core1[...]
 
 
+def pick(scratch, refs, ranges, head, wanted):
+    for ref, (first, end) in zip(refs, ranges):
+
+        @pl.when(wanted & (head >= first) & (head < end))
+        def _(ref=ref):
+            scratch[...] = ref[...]
+
+
 def forward_kernel(
     core_ref, d0, d1, d2, q, k0, kc, kd, k2, v0, vc, vd, v2, cot, gain,
     o, lse, stat, bias, k1, v1, squares, inner,
@@ -71,7 +80,8 @@
 
     @pl.when(h == 0)
     def _():
-        rows = [d[0:1, :] for d in (d0, d1, d2)]
+        near = jnp.where(core_ref[0] == 0, d2[8:9, :], d1[0:1, :])
+        rows = [d0[0:1, :], near, d2[0:1, :]]
         write_bias(bias, rows, [rows[0]] * 3, ("own", "near", "far"))
         squares[...] = jnp.zeros_like(squares)
         inner[...] = jnp.zeros_like(inner)
@@ -107,15 +117,14 @@
     return high, middle, (value - high - middle).astype(BF16).astype(F32)
 
 
-def norm_kernel(
-    features, chunks, docs, parts, lse, o, cot, gain, normed, own_stats, *rest,
-):
+def norm_kernel(features, chunks, count, docs, lse, o, cot, gain, *rest):
+    parts, (normed, own_stats, *rest) = rest[:count], rest[count:]
     pieces, (inv, coef, packed) = rest[:-3], rest[-3:]
     h = pl.program_id(0)
 
     @pl.when(h == 0)
     def _():
-        stat = parts[0:8, :] + parts[8:16, :] + parts[16:24, :] + parts[24:32, :]
+        stat = functools.reduce(jnp.add, [part[...] for part in parts])
         inverse = lax.rsqrt(stat[0:1, :] / features + 1e-05)
         inv[...] = as_columns(inverse)
         coef[...] = as_columns(inverse * inverse * inverse * stat[1:2, :] / features)
@@ -152,7 +161,8 @@
 
     @pl.when(h == 0)
     def _():
-        rows = [d[0:1, :] for d in (d0, d1, d2)]
+        near = jnp.where(core_ref[0] == 0, d2[8:9, :], d1[0:1, :])
+        rows = [d0[0:1, :], near, d2[0:1, :]]
         write_bias(bias, rows, [rows[0]] * 3, ("own", "near", "far"))
 
     for piece, (first, end) in zip(pieces, chunks):
@@ -178,31 +188,56 @@
     dq[...] = (total.T * SCALE).astype(BF16)
 
 
-def keys_kernel(
-    base, aliased, core_ref, docs, pc, pd, p2, k, v, qc, qd, q2, gc, gd, g2, dk0, dv0, *rest,
-):
-    if aliased:
-        rest = rest[2:]
-    dk, dv, bias, q1, g1, packed, s1, s2 = rest
+def keys_kernel(base, q_ranges, g_ranges, core_ref, *refs):
+    refs = list(refs)
+
+    def take(n):
+        taken = refs[:n]
+        del refs[:n]
+        return taken
+
+    later = base > 0
     h = pl.program_id(0)
-
-    @pl.when(h == 0)
-    def _():
-        choose(core_ref, packed, pc, pd)
-        for s, p in ((s1, packed), (s2, p2)):
-            parts = p[...].astype(F32).T
-            s[...] = parts[:STATS] + parts[STATS : 2 * STATS] + parts[2 * STATS : 3 * STATS]
-        rows = [s1[28:29, :], s2[28:29, :]]
-        write_bias(bias, [docs[0:1, :]] * 2, rows, ("near", "far"))
-
-    choose(core_ref, q1, qc, qd)
-    choose(core_ref, g1, gc, gd)
+    if later:
+        bias, s1, s2 = take(3)
+    else:
+        docs, pc, pd, p2 = take(4)
+    k, v, qc = take(3)
+    qds, q2s = take(len(q_ranges)), take(len(q_ranges))
+    gc, g2 = take(2)
+    gds = take(len(g_ranges))
+    dk0, dv0 = take(2)
+    if later:
+        take(2)
+    dk, dv = take(2)
+    if not later:
+        bias, s1, s2 = take(3)
+    q1, q2, g1, packed = refs
+
+    if not later:
+
+        @pl.when(h == 0)
+        def _():
+            choose(core_ref, packed, pc, pd)
+            for s, p in ((s1, packed), (s2, p2)):
+                parts = p[...].astype(F32).T
+                s[...] = parts[:STATS] + parts[STATS : 2 * STATS] + parts[2 * STATS : 3 * STATS]
+            rows = [s1[28:29, :], s2[28:29, :]]
+            write_bias(bias, [docs[0:1, :]] * 2, rows, ("near", "far"))
+
+    head = base + h
+    core0 = core_ref[0] == 0
+    pick(q2, q2s, q_ranges, head, True)
+    pick(q1, qds, q_ranges, head, core_ref[0] != 0)
+    pick(q1, [qc], [(0, head + 1)], head, core0)
+    pick(g1, gds, g_ranges, head, core_ref[0] != 0)
+    pick(g1, [gc], [(0, head + 1)], head, core0)
     key, value = k[...], v[...]
     grad_key, grad_value = dk0[...], dv0[...]
     for b, (q, g, stats) in enumerate(((q1, g1, s1), (q2, g2, s2))):
         query, out_grad = q[...], g[...]
-        lse = stats[pl.ds(base + h, 1), :]
-        delta = stats[pl.ds(16 + base + h, 1), :]
+        lse = stats[pl.ds(head, 1), :]
+        delta = stats[pl.ds(16 + head, 1), :]
         weights = jnp.exp2(dot_nt(key, query) * SCALE2 + bias[b] - lse)
         dscore = (weights * (dot_nt(value, out_grad) - delta)).astype(BF16)
         grad_key = grad_key + dot_nn(dscore, query)
@@ -227,7 +262,7 @@
     features = width * lax.axis_size("tp")
     section = lax.axis_index("section")
     core = lax.rem(section, 2).astype(jnp.int32).reshape(1)
-    ahead = {d: [(s, s + d) for s in range(count) if 0 <= s + d < count] for d in (1, 2, -2)}
+    ahead = {d: [(s, s + d) for s in range(count) if 0 <= s + d < count] for d in (2, -2)}
     to_core1 = [(s, s + 1) for s in range(0, count, 2)]
     to_core0 = [(s + 1, s) for s in range(0, count, 2)]
     gain = gain.reshape(1, width)
@@ -236,16 +271,18 @@
 
     k2 = send(keys, ahead[2])
     v2 = send(values, ahead[2])
-    d1 = send(d0, ahead[1])
-    d2 = send(d0, ahead[2])
-    kc = send(keys, to_core1)
-    vc = send(values, to_core1)
-    qc = send(queries, to_core0)
-    k2, kc, vc, qc, gain = lax.optimization_barrier((k2, kc, vc, qc, gain))
+    d1 = send(d0, to_core1 + to_core0)
+    d2 = send(jnp.concatenate([d0, d1], axis=0), ahead[2])
+    k2, *local = lax.optimization_barrier((k2, keys, values, queries))
     kd = send(k2, to_core0)
+    kc = send(local[0], to_core1)
+    vc = send(local[1], to_core1)
+    qc = send(local[2], to_core0)
     chunks = [(sum(CHUNKS[:i]), sum(CHUNKS[: i + 1])) for i in range(len(CHUNKS))]
-    q_first, q_last = [queries[:, a * HS : b * HS] for a, b in chunks]
-    v2, d1, d2, kd, q_first, q_last = lax.optimization_barrier((v2, d1, d2, kd, q_first, q_last))
+    q_first, q_last = queries[:, : QUERIES * HS], queries[:, QUERIES * HS :]
+    v2, d1, d2, kd, kc, vc, gain, q_first, q_last = lax.optimization_barrier(
+        (v2, d1, d2, kd, kc, vc, gain, q_first, q_last)
+    )
 
     q2a = send(q_first, ahead[-2])
     vd = send(v2, to_core0)
@@ -273,7 +310,7 @@
     attended, lse, stat = pl.pallas_call(
         forward_kernel,
         grid=(heads,),
-        in_specs=[smem] + [whole((8, rows))] * 3 + [head()] * 10 + [gain_head()],
+        in_specs=[smem] + [whole((8, rows))] * 2 + [whole((16, rows))] + [head()] * 10 + [gain_head()],
         out_specs=[head(), whole((16, rows)), whole((8, rows))],
         out_shape=[
             wide,
@@ -291,17 +328,21 @@
         **params(),
     )(core, d0, d1, d2, queries, keys, kc, kd, k2, values, vc, vd, v2, cotangent, gain)
 
-    parts = lax.all_gather(after(stat, q2a), "tp", tiled=True)
-    q_last = after(q_last, parts)
+    stat = after(stat, q2a)
+    tp = lax.axis_size("tp")
+    parts = [stat]
+    for step in range(1, tp):
+        parts.append(lax.ppermute(stat, "tp", [(i, (i + step) % tp) for i in range(tp)]))
+    q_last, *parts = lax.optimization_barrier((q_last, *parts))
     q2b = send(q_last, ahead[-2])
 
     widths = [(b - a) * HS for a, b in chunks]
     widths[0] += HS
     normed, stats, *pieces = pl.pallas_call(
-        functools.partial(norm_kernel, features, chunks),
+        functools.partial(norm_kernel, features, chunks, tp),
         grid=(heads,),
-        in_specs=[whole((8, rows)), whole((32, rows)), whole((16, rows))]
-        + [head(), head(), gain_head()],
+        in_specs=[whole((8, rows)), whole((16, rows)), head(), head(), gain_head()]
+        + [whole((8, rows))] * tp,
         out_specs=[head(), whole((STATS, rows)), whole((rows, widths[0]))]
         + [part(*chunk) for chunk in chunks[1:]],
         out_shape=[thin, jax.ShapeDtypeStruct((STATS, rows), F32)]
@@ -309,7 +350,7 @@
         scratch_shapes=[pltpu.VMEM((rows, HS), F32)] * 2 + [pltpu.VMEM((HS, rows), F32)],
         name="norm",
         **params(),
-    )(d0, parts, lse, attended, cotangent, gain)
+    )(d0, lse, attended, cotangent, gain, *parts)
 
     g2s = [send(piece, ahead[-2]) for piece in pieces]
     gcs = [send(piece, to_core0) for piece in pieces]
@@ -318,8 +359,8 @@
         functools.partial(own_kernel, chunks),
         grid=(heads,),
         in_specs=[smem]
-        + [whole((8, rows))] * 3
-        + [whole((STATS, rows))]
+        + [whole((8, rows))] * 2
+        + [whole((16, rows)), whole((STATS, rows))]
         + [head()] * 9
         + [part(*chunk) for chunk in chunks],
         out_specs=[head()] * 3,
@@ -332,48 +373,65 @@
     q2s = [q2a, q2b]
     qds = [send(q, to_core1) for q in lax.optimization_barrier((q2a, q2b, grad_query))[:2]]
     first = after(g2s[0], *qds)
-    out = ()
+    middle = CHUNKS[0]
+    gds = []
     for a, b in HANDED:
-        i = 0 if b <= CHUNKS[0] else 1
-        start = a - chunks[i][0]
-        if i == 0:
-            end = b if b < CHUNKS[0] else b + 1
-            gd = send(first[:, a * HS : end * HS], to_core1)
-            if b == CHUNKS[0]:
-                stats_at = b - a
-                pd = gd
-        else:
-            gd = send(after(g2s[1], *out), to_core1)
-        if a == 0:
-            waiting = gd
-            continue
-        steps = [(a, b, gd)]
-        if i == 0:
-            steps = [(0, a, waiting), (a, b, gd)]
-        for a, b, gd in steps:
-            start = a - chunks[i][0]
-            out = pl.pallas_call(
-                functools.partial(keys_kernel, a, len(out) > 0),
-                grid=(b - a,),
-                in_specs=[smem, whole((8, rows))]
-                + [stats_block(CHUNKS[0]), stats_block(stats_at), stats_block(CHUNKS[0])]
-                + [head(a)] * 3
-                + [head(start)] * 3
-                + [head(), head(start)]
-                + [head(a)] * 2
-                + [pl.BlockSpec(memory_space=pl.ANY)] * len(out),
-                out_specs=[head(a)] * 2,
-                out_shape=[thin, thin],
-                input_output_aliases={15: 0, 16: 1} if out else {},
-                scratch_shapes=[pltpu.VMEM((2, rows, rows), F32), tile, tile, tile]
-                + [pltpu.VMEM((STATS, rows), F32)] * 2,
-                name="keys",
-                **params(),
-            )(
-                core, d0, gcs[0], pd, g2s[0], keys, values, qc, qds[i], q2s[i],
-                gcs[i], gd, g2s[i], dk0, dv0, *out,
-            )
-    return normed, grad_query, out[0], out[1]
+        gds.append(send(first[:, a * HS : (b if b < middle else b + 1) * HS], to_core1))
+
+    def spread(base, ranges):
+        return [
+            pl.BlockSpec((rows, HS), lambda h, f=f, e=e: (0, jnp.clip(base + h, f, e - 1) - f))
+            for f, e in ranges
+        ]
+
+    q_ranges = [(0, QUERIES), (QUERIES, heads)]
+    both = [head()] * 2
+    bias_block = pl.BlockSpec((2, rows, rows), lambda h: (0, 0, 0))
+    stats_type = jax.ShapeDtypeStruct((STATS, rows), F32)
+    scratch = [tile] * 4
+    dk, dv, bias, s1, s2 = pl.pallas_call(
+        functools.partial(keys_kernel, 0, q_ranges, HANDED),
+        grid=(middle,),
+        in_specs=[smem, whole((8, rows)), stats_block(middle)]
+        + [stats_block(HANDED[-1][1] - HANDED[-1][0]), stats_block(middle)]
+        + [head()] * 3
+        + spread(0, q_ranges) * 2
+        + both
+        + spread(0, HANDED)
+        + both,
+        out_specs=both + [bias_block] + [whole((STATS, rows))] * 2,
+        out_shape=[thin, thin, jax.ShapeDtypeStruct((2, rows, rows), F32)] + [stats_type] * 2,
+        scratch_shapes=scratch,
+        name="keys",
+        **params(),
+    )(
+        core, d0, gcs[0], gds[-1], g2s[0], keys, values, qc, *qds, *q2s,
+        gcs[0], g2s[0], *gds, dk0, dv0,
+    )
+    gd = send(after(g2s[1], dk), to_core1)
+    rest = [(middle, heads)]
+    dk, dv = pl.pallas_call(
+        functools.partial(keys_kernel, middle, q_ranges[1:], rest),
+        grid=(heads - middle,),
+        in_specs=[smem, bias_block]
+        + [whole((STATS, rows))] * 2
+        + [head(middle)] * 3
+        + spread(middle, q_ranges[1:]) * 2
+        + both
+        + spread(middle, rest)
+        + [head(middle)] * 2
+        + [pl.BlockSpec(memory_space=pl.ANY)] * 2,
+        out_specs=[head(middle)] * 2,
+        out_shape=[thin, thin],
+        input_output_aliases={14: 0, 15: 1},
+        scratch_shapes=scratch,
+        name="keys",
+        **params(),
+    )(
+        core, bias, s1, s2, keys, values, qc, qds[1], q2s[1],
+        gcs[1], g2s[1], gd, dk0, dv0, dk, dv,
+    )
+    return normed, grad_query, dk, dv
 
 
 def solution(mesh):

time: 277 us -> 271 us (0.978)
  waiting for transfers between devices: 59.4 us -> 76.5 us
  starting transfers between devices: 126 us -> 114 us
  blocking collectives: 11.1 us -> 0 us
    ppermute x20 -> x21, waiting for transfers between devices: 59.4 us -> 74.6 us  [send(): return lax.ppermute(value, 'section', pairs)]
    ppermute x20 -> x21, starting transfers between devices: 126 us -> 111 us  [send(): return lax.ppermute(value, 'section', pairs)]
    all_gather x1 -> x0, blocking collectives: 11.1 us -> none  [body(): parts = lax.all_gather(after(stat, q2a), 'tp', tiled=True)]
    ppermute x0 -> x3, starting transfers between devices: none -> 3.27 us  [body(): lax.ppermute(stat, 'tp', [(i, (i + step) % tp) for i in range(tp)])]
    pallas_call x4 -> x3, Pallas kernels: 29.8 us -> 27.9 us  [the longest x1 9.35 us: body(): pl.pallas_call(functools.partial(keys_kernel, middle, q_ranges[1:], rest)...]
  transfers between devices with their start and end apart: 20 -> 24, of which waited for: 6 -> 10; matrix products, arithmetic and copies ran while one was open for 2% -> 2% of each run, Pallas kernels for 22% -> 22%
where the time goes in v2:
time: 271 us; the launch traced here: 269 us
  starting transfers between devices  114 us (42%)
  waiting for transfers between devices  76.5 us (28%)
  Pallas kernels  67.1 us (25%)
  local copies, waits for them, and re-layouts  9.09 us (3%)
    ppermute x21, starting transfers between devices, send(): return lax.ppermute(value, 'section', pairs)  111 us
    ppermute x21, waiting for transfers between devices, send(): return lax.ppermute(value, 'section', pairs)  74.6 us
    pallas_call x1, Pallas kernels, body(): pl.pallas_call(functools.partial(own_kernel, chunks), grid=(heads,), in_s...  20.3 us
    pallas_call x1, Pallas kernels, body(): pl.pallas_call(forward_kernel, grid=(heads,), in_specs=[smem] + [whole((8...  18.9 us
    pallas_call x1, Pallas kernels, body(): pl.pallas_call(functools.partial(keys_kernel, middle, q_ranges[1:], rest)...  9.35 us
    pallas_call x1, Pallas kernels, body(): pl.pallas_call(functools.partial(keys_kernel, 0, q_ranges, HANDED), grid=...  9.33 us
    pallas_call x1, Pallas kernels, body(): pl.pallas_call(functools.partial(norm_kernel, features, chunks, tp), grid...  9.26 us
  transfers between devices with their start and end apart: 24, of which 10 were waited for; matrix products, arithmetic and copies ran while one was open for 2% of the time, Pallas kernels for 22%

profile of v2, /device:TPU:5, one launch (start us, length us, event | category | flops | bytes accessed | tf_op | source)
XLA Modules:
  0.0 268.7 jit_solution(1865403288932369027)
XLA Ops:
  0.6 8.8 %collective-permute-start.3 = (bf16[384,1536]{1,0:T(8,128)(2,1)}, bf16[384,1536]{1,0:T(8,128)(2,1)S(1)}, u32[]{:S(2)}, u32[]{:S(2)}) collective-permute-start(bf16[384,1536]{1,0:T(8,128)(2,1)} %refs_3_.1), channel_id=1, source_target_pairs={{0,8},{4,12},{8,16},{12,20},{16,24},{20,28},{24,32},{28,36},{32,40... | collective-permute-start | bytes 3538952 | tf_op jit(solution)/shard_map/ppermute | solution.py:24
  9.5 1.9 collective-permute-start
  11.4 33.8 %collective-permute-done.3.k2 = bf16[384,1536]{1,0:T(8,128)(2,1)S(1)} collective-permute-done((bf16[384,1536]{1,0:T(8,128)(2,1)}, bf16[384,1536]{1,0:T(8,128)(2,1)S(1)}, u32[]{:S(2)}, u32[]{:S(2)}) %collective-permute-start.3) | collective-permute-done | bytes 1179680 | tf_op jit(solution)/shard_map/ppermute | solution.py:24
  45.2 4.2 %collective-permute-start.4 = (bf16[384,1536]{1,0:T(8,128)(2,1)S(1)}, bf16[384,1536]{1,0:T(8,128)(2,1)S(1)}, u32[]{:S(2)}, u32[]{:S(2)}) collective-permute-start(bf16[384,1536]{1,0:T(8,128)(2,1)S(1)} %collective-permute-done.3.k2), channel_id=1, source_target_pairs={{4,0},{12,8},{20,16},{28,24},{36,32},{44,40},{52,48},{60,56},{68,6... | collective-permute-start | bytes 3538952 | tf_op jit(solution)/shard_map/ppermute | solution.py:24
  49.4 1.3 collective-permute-start.5
  50.7 1.3 collective-permute-start.6
  54.0 1.9 collective-permute-done.1.d1
  55.9 5.0 %collective-permute-start.2 = (f32[16,384]{1,0:T(8,128)S(1)}, f32[16,384]{1,0:T(8,128)S(1)}, u32[]{:S(2)}, u32[]{:S(2)}) collective-permute-start(f32[16,384]{1,0:T(8,128)S(1)} %pad_maximum_fusion), channel_id=1, source_target_pairs={{0,8},{4,12},{8,16},{12,20},{16,24},{20,28},{24,32},{28,36},{32,40... | collective-permute-start | bytes 73736 | tf_op jit(solution)/shard_map/ppermute | solution.py:24
  62.0 2.0 slice.16
  64.6 19.1 %collective-permute-done.2.d2 = f32[16,384]{1,0:T(8,128)S(1)} collective-permute-done((f32[16,384]{1,0:T(8,128)S(1)}, f32[16,384]{1,0:T(8,128)S(1)}, u32[]{:S(2)}, u32[]{:S(2)}) %collective-permute-start.2) | collective-permute-done | bytes 24608 | tf_op jit(solution)/shard_map/ppermute | solution.py:24
  85.8 31.3 %collective-permute-start.7 = (bf16[384,1536]{1,0:T(8,128)(2,1)S(1)}, bf16[384,1536]{1,0:T(8,128)(2,1)S(1)}, u32[]{:S(2)}, u32[]{:S(2)}) collective-permute-start(bf16[384,1536]{1,0:T(8,128)(2,1)S(1)} %collective-permute-done.v2), channel_id=1, source_target_pairs={{4,0},{12,8},{20,16},{28,24},{36,32},{44,40},{52,48},{60,56},{68,6... | collective-permute-start | bytes 3538952 | tf_op jit(solution)/shard_map/ppermute | solution.py:24
  117.1 10.5 %collective-permute-start.8 = (bf16[384,640]{1,0:T(8,128)(2,1)S(1)}, bf16[384,640]{1,0:T(8,128)(2,1)S(1)}, u32[]{:S(2)}, u32[]{:S(2)}) collective-permute-start(bf16[384,640]{1,0:T(8,128)(2,1)S(1)} %slice.15), channel_id=1, source_target_pairs={{8,0},{12,4},{16,8},{20,12},{24,16},{28,20},{32,24},{36,28},{40,32... | collective-permute-start | bytes 1474568 | tf_op jit(solution)/shard_map/ppermute | solution.py:24
  128.8 18.9 %forward.1 = (f32[384,1536]{1,0:T(8,128)}, f32[16,384]{1,0:T(8,128)}, f32[8,384]{1,0:T(8,128)}) custom-call(s32[1]{0:T(128)} %bitcast.core_ref, f32[8,384]{1,0:T(8,128)} %copy-done.14, f32[8,384]{1,0:T(8,128)} %copy-done.17, f32[16,384]{1,0:T(8,128)} %copy-done.18, bf16[384,1536]{1,0:T(8,128)(2,1)} %q.3, bf16[384,1536]{1,0:T(8,128)(2,1)} %refs_3_.1, ...), custom_call_target="tpu_custom_call" | custom-call | tf_op jit(solution)/shard_map/forward/pallas_call | solution.py:310
  149.7 2.6 collective-permute-start.11
  154.2 10.9 %collective-permute-start.14 = (bf16[384,896]{1,0:T(8,128)(2,1)}, bf16[384,896]{1,0:T(8,128)(2,1)S(1)}, u32[]{:S(2)}, u32[]{:S(2)}) collective-permute-start(bf16[384,896]{1,0:T(8,128)(2,1)} %slice.16), channel_id=1, source_target_pairs={{8,0},{12,4},{16,8},{20,12},{24,16},{28,20},{32,24},{36,28},{40,32... | collective-permute-start | bytes 2064392 | tf_op jit(solution)/shard_map/ppermute | solution.py:24
  165.1 3.9 %collective-permute-start.18 = (bf16[384,1536]{1,0:T(8,128)(2,1)S(1)}, bf16[384,1536]{1,0:T(8,128)(2,1)S(1)}, u32[]{:S(2)}, u32[]{:S(2)}) collective-permute-start(bf16[384,1536]{1,0:T(8,128)(2,1)S(1)} %copy-done), channel_id=1, source_target_pairs={{4,0},{12,8},{20,16},{28,24},{36,32},{44,40},{52,48},{60,56},{68,6... | collective-permute-start | bytes 3538952 | tf_op jit(solution)/shard_map/ppermute | solution.py:24
  169.0 9.3 %norm.1 = (bf16[384,1536]{1,0:T(8,128)(2,1)}, f32[32,384]{1,0:T(8,128)}, bf16[384,896]{1,0:T(8,128)(2,1)}, bf16[384,768]{1,0:T(8,128)(2,1)}) custom-call(f32[8,384]{1,0:T(8,128)} %copy-done.14, f32[16,384]{1,0:T(8,128)} %get-tuple-element.54.lse, f32[384,1536]{1,0:T(8,128)} %get-tuple-element.55.o, bf16[384,1536]{1,0:T(8,128)(2,1)} %cot.3, ...), custom_call_target="tpu_custom_call" | custom-call | tf_op jit(solution)/shard_map/norm/pallas_call | solution.py:341
  178.2 1.9 collective-permute-start.13
  180.2 20.3 %own.1 = (bf16[384,1536]{1,0:T(8,128)(2,1)}, f32[384,1536]{1,0:T(8,128)}, f32[384,1536]{1,0:T(8,128)}) custom-call(s32[1]{0:T(128)} %bitcast.core_ref, f32[8,384]{1,0:T(8,128)} %copy-done.14, f32[8,384]{1,0:T(8,128)} %copy-done.17, f32[16,384]{1,0:T(8,128)} %copy-done.18, f32[32,384]{1,0:T(8,128)} %get-tuple-element.65.stats, bf16[384,1536]{1,0:T(8,128)(2,1)} %q.3, ...), custom_call_target="tpu_custom_call" | custom-call | tf_op jit(solution)/shard_map/own/pallas_call | solution.py:358
  200.4 6.0 %collective-permute-done.14.refs_10_.refs_7_ = bf16[384,896]{1,0:T(8,128)(2,1)S(1)} collective-permute-done((bf16[384,896]{1,0:T(8,128)(2,1)}, bf16[384,896]{1,0:T(8,128)(2,1)S(1)}, u32[]{:S(2)}, u32[]{:S(2)}) %collective-permute-start.14) | collective-permute-done | bytes 688160 | tf_op jit(solution)/shard_map/ppermute | solution.py:24
  207.8 1.3 collective-permute-start.15
  209.1 9.1 %collective-permute-start.12 = (bf16[384,896]{1,0:T(8,128)(2,1)}, bf16[384,896]{1,0:T(8,128)(2,1)}, u32[]{:S(2)}, u32[]{:S(2)}) collective-permute-start(bf16[384,896]{1,0:T(8,128)(2,1)} %get-tuple-element.66.rest_0_), channel_id=1, source_target_pairs={{4,0},{12,8},{20,16},{28,24},{36,32},{44,40},{52,48},{60,56},{68,6... | collective-permute-start | bytes 2064392 | tf_op jit(solution)/shard_map/ppermute | solution.py:24
  218.2 7.0 %collective-permute-done.13.refs_3_.refs_12_ = bf16[384,896]{1,0:T(8,128)(2,1)S(1)} collective-permute-done((bf16[384,896]{1,0:T(8,128)(2,1)}, bf16[384,896]{1,0:T(8,128)(2,1)S(1)}, u32[]{:S(2)}, u32[]{:S(2)}) %collective-permute-start.13) | collective-permute-done | bytes 688160 | tf_op jit(solution)/shard_map/ppermute | solution.py:24
  225.2 7.0 %collective-permute-start.22 = (bf16[384,768]{1,0:T(8,128)(2,1)}, bf16[384,768]{1,0:T(8,128)(2,1)}, u32[]{:S(2)}, u32[]{:S(2)}) collective-permute-start(bf16[384,768]{1,0:T(8,128)(2,1)} %get-tuple-element.67.rest_1_), channel_id=1, source_target_pairs={{8,0},{12,4},{16,8},{20,12},{24,16},{28,20},{32,24},{36,28},{40,32... | collective-permute-start | bytes 1769480 | tf_op jit(solution)/shard_map/ppermute | solution.py:24
  232.2 1.3 collective-permute-start.17
  233.6 1.3 collective-permute-start.19
  234.9 1.3 collective-permute-start.20
  236.2 4.9 %collective-permute-start.21 = (bf16[384,768]{1,0:T(8,128)(2,1)}, bf16[384,768]{1,0:T(8,128)(2,1)S(1)}, u32[]{:S(2)}, u32[]{:S(2)}) collective-permute-start(bf16[384,768]{1,0:T(8,128)(2,1)} %get-tuple-element.67.rest_1_), channel_id=1, source_target_pairs={{4,0},{12,8},{20,16},{28,24},{36,32},{44,40},{52,48},{60,56},{68,6... | collective-permute-start | bytes 1769480 | tf_op jit(solution)/shard_map/ppermute | solution.py:24
  242.5 9.3 %keys.2 = (bf16[384,1536]{1,0:T(8,128)(2,1)}, bf16[384,1536]{1,0:T(8,128)(2,1)}, f32[2,384,384]{2,1,0:T(8,128)}, f32[32,384]{1,0:T(8,128)}, f32[32,384]{1,0:T(8,128)}) custom-call(s32[1]{0:T(128)} %bitcast.core_ref, f32[8,384]{1,0:T(8,128)} %copy-done.14, bf16[384,896]{1,0:T(8,128)(2,1)} %collective-permute-done.12.refs_1_.refs_11_, ...), custom_call_target="tpu_custom_call" | custom-call | tf_op jit(solution)/shard_map/keys/pallas_call | solution.py:392
  251.9 2.6 collective-permute-done.22.refs_9_
  255.7 2.8 %collective-permute-done.23.refs_10_ = bf16[384,768]{1,0:T(8,128)(2,1)S(1)} collective-permute-done((bf16[384,768]{1,0:T(8,128)(2,1)}, bf16[384,768]{1,0:T(8,128)(2,1)S(1)}, u32[]{:S(2)}, u32[]{:S(2)}) %collective-permute-start.23) | collective-permute-done | bytes 589856 | tf_op jit(solution)/shard_map/ppermute | solution.py:24
  259.3 9.3 %keys.3 = (bf16[384,1536]{1,0:T(8,128)(2,1)}, bf16[384,1536]{1,0:T(8,128)(2,1)}) custom-call(s32[1]{0:T(128)} %bitcast.core_ref, f32[2,384,384]{2,1,0:T(8,128)} %get-tuple-element.76.refs_0_, f32[32,384]{1,0:T(8,128)} %get-tuple-element.77.refs_1_, f32[32,384]{1,0:T(8,128)} %get-tuple-element.78.refs_2_, ...), custom_call_target="tpu_custom_call", output_to_operand_aliasing={{0}: (14, {}), {1}: (15, {})} | custom-call | tf_op jit(solution)/shard_map/keys/pallas_call | solution.py:413
  (75 shorter events, 15.5 us)
Async XLA Ops:
  0.6 44.6 %collective-permute-start.3 = (bf16[384,1536]{1,0:T(8,128)(2,1)}, bf16[384,1536]{1,0:T(8,128)(2,1)S(1)}, u32[]{:S(2)}, u32[]{:S(2)}) collective-permute-start(bf16[384,1536]{1,0:T(8,128)(2,1)} %refs_3_.1), channel_id=1, source_target_pairs={{0,8},{4,12},{8,16},{12,20},{16,24},{20,28},{24,32},{28,36},{32,40... | collective-permute-start | bytes 3538952 | tf_op jit(solution)/shard_map/ppermute | solution.py:24
  9.5 74.3 %collective-permute-start = (bf16[384,1536]{1,0:T(8,128)(2,1)}, bf16[384,1536]{1,0:T(8,128)(2,1)S(1)}, u32[]{:S(2)}, u32[]{:S(2)}) collective-permute-start(bf16[384,1536]{1,0:T(8,128)(2,1)} %refs_4_.3), channel_id=1, source_target_pairs={{0,8},{4,12},{8,16},{12,20},{16,24},{20,28},{24,32},{28,36},{32,40... | collective-permute-start | bytes 3538952 | tf_op jit(solution)/shard_map/ppermute | solution.py:24
  45.2 18.8 %copy-start.2 = (bf16[384,1536]{1,0:T(8,128)(2,1)}, bf16[384,1536]{1,0:T(8,128)(2,1)S(1)}, u32[]{:S(2)}) copy-start(bf16[384,1536]{1,0:T(8,128)(2,1)S(1)} %collective-permute-done.3.k2) | copy-start | bytes 3538948
  45.2 38.6 %collective-permute-start.4 = (bf16[384,1536]{1,0:T(8,128)(2,1)S(1)}, bf16[384,1536]{1,0:T(8,128)(2,1)S(1)}, u32[]{:S(2)}, u32[]{:S(2)}) collective-permute-start(bf16[384,1536]{1,0:T(8,128)(2,1)S(1)} %collective-permute-done.3.k2), channel_id=1, source_target_pairs={{4,0},{12,8},{20,16},{28,24},{36,32},{44,40},{52,48},{60,56},{68,6... | collective-permute-start | bytes 3538952 | tf_op jit(solution)/shard_map/ppermute | solution.py:24
  49.4 34.4 %collective-permute-start.5 = (bf16[384,1536]{1,0:T(8,128)(2,1)}, bf16[384,1536]{1,0:T(8,128)(2,1)S(1)}, u32[]{:S(2)}, u32[]{:S(2)}) collective-permute-start(bf16[384,1536]{1,0:T(8,128)(2,1)} %refs_3_.1), channel_id=1, source_target_pairs={{0,4},{8,12},{16,20},{24,28},{32,36},{40,44},{48,52},{56,60},{64,6... | collective-permute-start | bytes 3538952 | tf_op jit(solution)/shard_map/ppermute | solution.py:24
  50.7 34.1 %collective-permute-start.6 = (bf16[384,1536]{1,0:T(8,128)(2,1)}, bf16[384,1536]{1,0:T(8,128)(2,1)S(1)}, u32[]{:S(2)}, u32[]{:S(2)}) collective-permute-start(bf16[384,1536]{1,0:T(8,128)(2,1)} %refs_4_.3), channel_id=1, source_target_pairs={{0,4},{8,12},{16,20},{24,28},{32,36},{40,44},{48,52},{56,60},{64,6... | collective-permute-start | bytes 3538952 | tf_op jit(solution)/shard_map/ppermute | solution.py:24
  52.7 3.2 %collective-permute-start.1 = (f32[8,384]{1,0:T(8,128)S(1)}, f32[8,384]{1,0:T(8,128)S(1)}, u32[]{:S(2)}, u32[]{:S(2)}) collective-permute-start(f32[8,384]{1,0:T(8,128)S(1)} %broadcast_in_dim.2.d0.docs.refs_0_), channel_id=1, source_target_pairs={{0,4},{8,12},{16,20},{24,28},{32,36},{40,44},{48,52},{56,60},{64,6... | collective-permute-start | bytes 36872 | tf_op jit(solution)/shard_map/ppermute | solution.py:24
  55.9 27.9 %collective-permute-start.2 = (f32[16,384]{1,0:T(8,128)S(1)}, f32[16,384]{1,0:T(8,128)S(1)}, u32[]{:S(2)}, u32[]{:S(2)}) collective-permute-start(f32[16,384]{1,0:T(8,128)S(1)} %pad_maximum_fusion), channel_id=1, source_target_pairs={{0,8},{4,12},{8,16},{12,20},{16,24},{20,28},{24,32},{28,36},{32,40... | collective-permute-start | bytes 73736 | tf_op jit(solution)/shard_map/ppermute | solution.py:24
  83.8 43.9 %copy-start.18 = (f32[16,384]{1,0:T(8,128)}, f32[16,384]{1,0:T(8,128)S(1)}, u32[]{:S(2)}) copy-start(f32[16,384]{1,0:T(8,128)S(1)} %collective-permute-done.2.d2) | copy-start | bytes 73732
  83.8 43.9 %copy-start.3 = (bf16[384,1536]{1,0:T(8,128)(2,1)}, bf16[384,1536]{1,0:T(8,128)(2,1)S(1)}, u32[]{:S(2)}) copy-start(bf16[384,1536]{1,0:T(8,128)(2,1)S(1)} %collective-permute-done.v2) | copy-start | bytes 3538948
  85.8 31.3 %copy-start.7 = (bf16[384,1536]{1,0:T(8,128)(2,1)}, bf16[384,1536]{1,0:T(8,128)(2,1)S(1)}, u32[]{:S(2)}) copy-start(bf16[384,1536]{1,0:T(8,128)(2,1)S(1)} %collective-permute-done.6.vc) | copy-start | bytes 3538948
  85.8 41.8 %collective-permute-start.7 = (bf16[384,1536]{1,0:T(8,128)(2,1)S(1)}, bf16[384,1536]{1,0:T(8,128)(2,1)S(1)}, u32[]{:S(2)}, u32[]{:S(2)}) collective-permute-start(bf16[384,1536]{1,0:T(8,128)(2,1)S(1)} %collective-permute-done.v2), channel_id=1, source_target_pairs={{4,0},{12,8},{20,16},{28,24},{36,32},{44,40},{52,48},{60,56},{68,6... | collective-permute-start | bytes 3538952 | tf_op jit(solution)/shard_map/ppermute | solution.py:24
  117.1 31.8 %collective-permute-start.8 = (bf16[384,640]{1,0:T(8,128)(2,1)S(1)}, bf16[384,640]{1,0:T(8,128)(2,1)S(1)}, u32[]{:S(2)}, u32[]{:S(2)}) collective-permute-start(bf16[384,640]{1,0:T(8,128)(2,1)S(1)} %slice.15), channel_id=1, source_target_pairs={{8,0},{12,4},{16,8},{20,12},{24,16},{28,20},{32,24},{36,28},{40,32... | collective-permute-start | bytes 1474568 | tf_op jit(solution)/shard_map/ppermute | solution.py:24
  128.8 36.3 %copy-start = (bf16[384,1536]{1,0:T(8,128)(2,1)S(1)}, bf16[384,1536]{1,0:T(8,128)(2,1)}, u32[]{:S(2)}) copy-start(bf16[384,1536]{1,0:T(8,128)(2,1)} %q.3) | copy-start | bytes 3538948
  149.0 29.2 %copy-start.13 = (bf16[384,640]{1,0:T(8,128)(2,1)}, bf16[384,640]{1,0:T(8,128)(2,1)S(1)}, u32[]{:S(2)}) copy-start(bf16[384,640]{1,0:T(8,128)(2,1)S(1)} %collective-permute-done.8.refs_9_) | copy-start | bytes 1474564
  149.0 4.6 %collective-permute-start.9 = (f32[8,384]{1,0:T(8,128)}, f32[8,384]{1,0:T(8,128)S(1)}, u32[]{:S(2)}, u32[]{:S(2)}) collective-permute-start(f32[8,384]{1,0:T(8,128)} %get-tuple-element.60.rest_0_), channel_id=1, source_target_pairs={{0,1},{1,2},{2,3},{3,0},{4,5},{5,6},{6,7},{7,4},{8,9},{9,10},{10,1... | collective-permute-start | bytes 36872 | tf_op jit(solution)/shard_map/ppermute | solution.py:335
  149.7 3.9 %collective-permute-start.10 = (f32[8,384]{1,0:T(8,128)}, f32[8,384]{1,0:T(8,128)S(1)}, u32[]{:S(2)}, u32[]{:S(2)}) collective-permute-start(f32[8,384]{1,0:T(8,128)} %get-tuple-element.60.rest_0_), channel_id=1, source_target_pairs={{0,2},{1,3},{2,0},{3,1},{4,6},{5,7},{6,4},{7,5},{8,10},{9,11},{10,... | collective-permute-start | bytes 36872 | tf_op jit(solution)/shard_map/ppermute | solution.py:335
  149.7 4.5 %collective-permute-start.11 = (f32[8,384]{1,0:T(8,128)}, f32[8,384]{1,0:T(8,128)S(1)}, u32[]{:S(2)}, u32[]{:S(2)}) collective-permute-start(f32[8,384]{1,0:T(8,128)} %get-tuple-element.60.rest_0_), channel_id=1, source_target_pairs={{0,3},{1,0},{2,1},{3,2},{4,7},{5,4},{6,5},{7,6},{8,11},{9,8},{10,9... | collective-permute-start | bytes 36872 | tf_op jit(solution)/shard_map/ppermute | solution.py:335
  154.2 52.3 %collective-permute-start.14 = (bf16[384,896]{1,0:T(8,128)(2,1)}, bf16[384,896]{1,0:T(8,128)(2,1)S(1)}, u32[]{:S(2)}, u32[]{:S(2)}) collective-permute-start(bf16[384,896]{1,0:T(8,128)(2,1)} %slice.16), channel_id=1, source_target_pairs={{8,0},{12,4},{16,8},{20,12},{24,16},{28,20},{32,24},{36,28},{40,32... | collective-permute-start | bytes 2064392 | tf_op jit(solution)/shard_map/ppermute | solution.py:24
  165.1 69.8 %collective-permute-start.18 = (bf16[384,1536]{1,0:T(8,128)(2,1)S(1)}, bf16[384,1536]{1,0:T(8,128)(2,1)S(1)}, u32[]{:S(2)}, u32[]{:S(2)}) collective-permute-start(bf16[384,1536]{1,0:T(8,128)(2,1)S(1)} %copy-done), channel_id=1, source_target_pairs={{4,0},{12,8},{20,16},{28,24},{36,32},{44,40},{52,48},{60,56},{68,6... | collective-permute-start | bytes 3538952 | tf_op jit(solution)/shard_map/ppermute | solution.py:24
  178.2 47.0 %collective-permute-start.13 = (bf16[384,896]{1,0:T(8,128)(2,1)}, bf16[384,896]{1,0:T(8,128)(2,1)S(1)}, u32[]{:S(2)}, u32[]{:S(2)}) collective-permute-start(bf16[384,896]{1,0:T(8,128)(2,1)} %get-tuple-element.66.rest_0_), channel_id=1, source_target_pairs={{8,0},{12,4},{16,8},{20,12},{24,16},{28,20},{32,24},{36,28},{40,32... | collective-permute-start | bytes 2064392 | tf_op jit(solution)/shard_map/ppermute | solution.py:24
  206.5 35.3 %copy-start.9 = (bf16[384,896]{1,0:T(8,128)(2,1)}, bf16[384,896]{1,0:T(8,128)(2,1)S(1)}, u32[]{:S(2)}) copy-start(bf16[384,896]{1,0:T(8,128)(2,1)S(1)} %collective-permute-done.14.refs_10_.refs_7_) | copy-start | bytes 2064388
  206.5 25.7 %collective-permute-start.16 = (bf16[384,896]{1,0:T(8,128)(2,1)S(1)}, bf16[384,896]{1,0:T(8,128)(2,1)}, u32[]{:S(2)}, u32[]{:S(2)}) collective-permute-start(bf16[384,896]{1,0:T(8,128)(2,1)S(1)} %collective-permute-done.14.refs_10_.refs_7_), channel_id=1, source_target_pairs={{0,4},{8,12},{16,20},{24,28},{32,36},{40,44},{48,52},{56,60},{64,6... | collective-permute-start | bytes 2064392 | tf_op jit(solution)/shard_map/ppermute | solution.py:24
  207.8 24.4 %collective-permute-start.15 = (bf16[384,640]{1,0:T(8,128)(2,1)}, bf16[384,640]{1,0:T(8,128)(2,1)}, u32[]{:S(2)}, u32[]{:S(2)}) collective-permute-start(bf16[384,640]{1,0:T(8,128)(2,1)} %copy-done.13), channel_id=1, source_target_pairs={{0,4},{8,12},{16,20},{24,28},{32,36},{40,44},{48,52},{56,60},{64,6... | collective-permute-start | bytes 1474568 | tf_op jit(solution)/shard_map/ppermute | solution.py:24
  209.1 27.1 %collective-permute-start.12 = (bf16[384,896]{1,0:T(8,128)(2,1)}, bf16[384,896]{1,0:T(8,128)(2,1)}, u32[]{:S(2)}, u32[]{:S(2)}) collective-permute-start(bf16[384,896]{1,0:T(8,128)(2,1)} %get-tuple-element.66.rest_0_), channel_id=1, source_target_pairs={{4,0},{12,8},{20,16},{28,24},{36,32},{44,40},{52,48},{60,56},{68,6... | collective-permute-start | bytes 2064392 | tf_op jit(solution)/shard_map/ppermute | solution.py:24
  225.2 16.6 %copy-start.1 = (bf16[384,896]{1,0:T(8,128)(2,1)}, bf16[384,896]{1,0:T(8,128)(2,1)S(1)}, u32[]{:S(2)}) copy-start(bf16[384,896]{1,0:T(8,128)(2,1)S(1)} %collective-permute-done.13.refs_3_.refs_12_) | copy-start | bytes 2064388
  225.2 29.2 %collective-permute-start.22 = (bf16[384,768]{1,0:T(8,128)(2,1)}, bf16[384,768]{1,0:T(8,128)(2,1)}, u32[]{:S(2)}, u32[]{:S(2)}) collective-permute-start(bf16[384,768]{1,0:T(8,128)(2,1)} %get-tuple-element.67.rest_1_), channel_id=1, source_target_pairs={{8,0},{12,4},{16,8},{20,12},{24,16},{28,20},{32,24},{36,28},{40,32... | collective-permute-start | bytes 1769480 | tf_op jit(solution)/shard_map/ppermute | solution.py:24
  232.2 8.9 %collective-permute-start.17 = (bf16[384,384]{1,0:T(8,128)(2,1)S(1)}, bf16[384,384]{1,0:T(8,128)(2,1)S(1)}, u32[]{:S(2)}, u32[]{:S(2)}) collective-permute-start(bf16[384,384]{1,0:T(8,128)(2,1)S(1)} %slice.17), channel_id=1, source_target_pairs={{0,4},{8,12},{16,20},{24,28},{32,36},{40,44},{48,52},{56,60},{64,6... | collective-permute-start | bytes 884744 | tf_op jit(solution)/shard_map/ppermute | solution.py:24
  233.6 7.5 %collective-permute-start.19 = (bf16[384,256]{1,0:T(8,128)(2,1)S(1)}, bf16[384,256]{1,0:T(8,128)(2,1)S(1)}, u32[]{:S(2)}, u32[]{:S(2)}) collective-permute-start(bf16[384,256]{1,0:T(8,128)(2,1)S(1)} %get-tuple-element.85), channel_id=1, source_target_pairs={{0,4},{8,12},{16,20},{24,28},{32,36},{40,44},{48,52},{56,60},{64,6... | collective-permute-start | bytes 589832 | tf_op jit(solution)/shard_map/ppermute | solution.py:24
  234.9 6.2 %collective-permute-start.20 = (bf16[384,256]{1,0:T(8,128)(2,1)S(1)}, bf16[384,256]{1,0:T(8,128)(2,1)S(1)}, u32[]{:S(2)}, u32[]{:S(2)}) collective-permute-start(bf16[384,256]{1,0:T(8,128)(2,1)S(1)} %get-tuple-element.84), channel_id=1, source_target_pairs={{0,4},{8,12},{16,20},{24,28},{32,36},{40,44},{48,52},{56,60},{64,6... | collective-permute-start | bytes 589832 | tf_op jit(solution)/shard_map/ppermute | solution.py:24
  236.2 19.5 %collective-permute-start.21 = (bf16[384,768]{1,0:T(8,128)(2,1)}, bf16[384,768]{1,0:T(8,128)(2,1)S(1)}, u32[]{:S(2)}, u32[]{:S(2)}) collective-permute-start(bf16[384,768]{1,0:T(8,128)(2,1)} %get-tuple-element.67.rest_1_), channel_id=1, source_target_pairs={{4,0},{12,8},{20,16},{28,24},{36,32},{44,40},{52,48},{60,56},{68,6... | collective-permute-start | bytes 1769480 | tf_op jit(solution)/shard_map/ppermute | solution.py:24
  254.4 4.1 %collective-permute-start.23 = (bf16[384,768]{1,0:T(8,128)(2,1)}, bf16[384,768]{1,0:T(8,128)(2,1)S(1)}, u32[]{:S(2)}, u32[]{:S(2)}) collective-permute-start(bf16[384,768]{1,0:T(8,128)(2,1)} %collective-permute-done.22.refs_9_), channel_id=1, source_target_pairs={{0,4},{8,12},{16,20},{24,28},{32,36},{40,44},{48,52},{56,60},{64,6... | collective-permute-start | bytes 1769480 | tf_op jit(solution)/shard_map/ppermute | solution.py:24
  (15 other events, 89.1 us)

commit v3 on v2

--- a/solution.py
+++ b/solution.py
@@ -13,7 +13,7 @@
 SCALE2 = SCALE * math.log2(math.e)
 HIDDEN = -1e30
 CHUNKS = (6, 6)
-HANDED = ((0, 2), (2, 4), (4, 6))
+HANDED = ((0, 3), (3, 6))
 QUERIES = 5
 STATS = 32
 F32 = jnp.float32
@@ -280,8 +280,8 @@
     qc = send(local[2], to_core0)
     chunks = [(sum(CHUNKS[:i]), sum(CHUNKS[: i + 1])) for i in range(len(CHUNKS))]
     q_first, q_last = queries[:, : QUERIES * HS], queries[:, QUERIES * HS :]
-    v2, d1, d2, kd, kc, vc, gain, q_first, q_last = lax.optimization_barrier(
-        (v2, d1, d2, kd, kc, vc, gain, q_first, q_last)
+    v2, d1, d2, kd, kc, vc, qc, gain, q_first, q_last = lax.optimization_barrier(
+        (v2, d1, d2, kd, kc, vc, qc, gain, q_first, q_last)
     )
 
     q2a = send(q_first, ahead[-2])

time: 271 us -> 271 us (level)
  starting transfers between devices: 114 us -> 125 us
  waiting for transfers between devices: 76.5 us -> 67.7 us
    ppermute x21 -> x20, starting transfers between devices: 111 us -> 123 us  [send(): return lax.ppermute(value, 'section', pairs)]
    ppermute x21 -> x20, waiting for transfers between devices: 74.6 us -> 63.1 us  [send(): return lax.ppermute(value, 'section', pairs)]
  transfers between devices with their start and end apart: 24 -> 23, of which waited for: 10 -> 9; matrix products, arithmetic and copies ran while one was open for 2% -> 1% of each run, Pallas kernels for 22% -> 21%
where the time goes in v3:
time: 271 us; the launch traced here: 269 us
  starting transfers between devices  125 us (46%)
  waiting for transfers between devices  67.7 us (25%)
  Pallas kernels  67.2 us (25%)
  local copies, waits for them, and re-layouts  8.05 us (3%)
    ppermute x20, starting transfers between devices, send(): return lax.ppermute(value, 'section', pairs)  123 us
    ppermute x20, waiting for transfers between devices, send(): return lax.ppermute(value, 'section', pairs)  63.1 us
    pallas_call x1, Pallas kernels, body(): pl.pallas_call(functools.partial(own_kernel, chunks), grid=(heads,), in_s...  20.3 us
    pallas_call x1, Pallas kernels, body(): pl.pallas_call(forward_kernel, grid=(heads,), in_specs=[smem] + [whole((8...  18.9 us
    pallas_call x1, Pallas kernels, body(): pl.pallas_call(functools.partial(keys_kernel, 0, q_ranges, HANDED), grid=...  9.37 us
    pallas_call x1, Pallas kernels, body(): pl.pallas_call(functools.partial(keys_kernel, middle, q_ranges[1:], rest)...  9.35 us
    pallas_call x1, Pallas kernels, body(): pl.pallas_call(functools.partial(norm_kernel, features, chunks, tp), grid...  9.28 us
  transfers between devices with their start and end apart: 23, of which 9 were waited for; matrix products, arithmetic and copies ran while one was open for 1% of the time, Pallas kernels for 21%

profile of v3, /device:TPU:5, one launch (start us, length us, event | category | flops | bytes accessed | tf_op | source)
XLA Modules:
  0.0 269.3 jit_solution(5378787415778241211)
XLA Ops:
  0.6 8.8 %collective-permute-start.3 = (bf16[384,1536]{1,0:T(8,128)(2,1)}, bf16[384,1536]{1,0:T(8,128)(2,1)S(1)}, u32[]{:S(2)}, u32[]{:S(2)}) collective-permute-start(bf16[384,1536]{1,0:T(8,128)(2,1)} %refs_3_.1), channel_id=1, source_target_pairs={{0,8},{4,12},{8,16},{12,20},{16,24},{20,28},{24,32},{28,36},{32,40... | collective-permute-start | bytes 3538952 | tf_op jit(solution)/shard_map/ppermute | solution.py:24
  11.9 2.0 collective-permute-start.2
  14.0 8.3 %collective-permute-start = (bf16[384,1536]{1,0:T(8,128)(2,1)}, bf16[384,1536]{1,0:T(8,128)(2,1)}, u32[]{:S(2)}, u32[]{:S(2)}) collective-permute-start(bf16[384,1536]{1,0:T(8,128)(2,1)} %refs_4_.3), channel_id=1, source_target_pairs={{0,8},{4,12},{8,16},{12,20},{16,24},{20,28},{24,32},{28,36},{32,40... | collective-permute-start | bytes 3538952 | tf_op jit(solution)/shard_map/ppermute | solution.py:24
  22.3 22.9 %collective-permute-done.3.k2 = bf16[384,1536]{1,0:T(8,128)(2,1)S(1)} collective-permute-done((bf16[384,1536]{1,0:T(8,128)(2,1)}, bf16[384,1536]{1,0:T(8,128)(2,1)S(1)}, u32[]{:S(2)}, u32[]{:S(2)}) %collective-permute-start.3) | collective-permute-done | bytes 1179680 | tf_op jit(solution)/shard_map/ppermute | solution.py:24
  45.2 1.3 collective-permute-start.5
  46.5 1.3 collective-permute-start.6
  47.8 4.3 %collective-permute-start.7 = (bf16[384,1536]{1,0:T(8,128)(2,1)}, bf16[384,1536]{1,0:T(8,128)(2,1)S(1)}, u32[]{:S(2)}, u32[]{:S(2)}) collective-permute-start(bf16[384,1536]{1,0:T(8,128)(2,1)} %q.3), channel_id=1, source_target_pairs={{4,0},{12,8},{20,16},{28,24},{36,32},{44,40},{52,48},{60,56},{68,6... | collective-permute-start | bytes 3538952 | tf_op jit(solution)/shard_map/ppermute | solution.py:24
  52.2 1.4 collective-permute-start.4
  54.6 1.2 slice.13
  56.4 27.5 %collective-permute-done.v2 = bf16[384,1536]{1,0:T(8,128)(2,1)} collective-permute-done((bf16[384,1536]{1,0:T(8,128)(2,1)}, bf16[384,1536]{1,0:T(8,128)(2,1)}, u32[]{:S(2)}, u32[]{:S(2)}) %collective-permute-start) | collective-permute-done | bytes 1179680 | tf_op jit(solution)/shard_map/ppermute | solution.py:24
  84.9 31.3 %collective-permute-start.8 = (bf16[384,1536]{1,0:T(8,128)(2,1)}, bf16[384,1536]{1,0:T(8,128)(2,1)S(1)}, u32[]{:S(2)}, u32[]{:S(2)}) collective-permute-start(bf16[384,1536]{1,0:T(8,128)(2,1)} %collective-permute-done.v2), channel_id=1, source_target_pairs={{4,0},{12,8},{20,16},{28,24},{36,32},{44,40},{52,48},{60,56},{68,6... | collective-permute-start | bytes 3538952 | tf_op jit(solution)/shard_map/ppermute | solution.py:24
  116.2 10.5 %collective-permute-start.9 = (bf16[384,640]{1,0:T(8,128)(2,1)S(1)}, bf16[384,640]{1,0:T(8,128)(2,1)}, u32[]{:S(2)}, u32[]{:S(2)}) collective-permute-start(bf16[384,640]{1,0:T(8,128)(2,1)S(1)} %slice.12), channel_id=1, source_target_pairs={{8,0},{12,4},{16,8},{20,12},{24,16},{28,20},{32,24},{36,28},{40,32... | collective-permute-start | bytes 1474568 | tf_op jit(solution)/shard_map/ppermute | solution.py:24
  127.8 18.9 %forward.1 = (f32[384,1536]{1,0:T(8,128)}, f32[16,384]{1,0:T(8,128)}, f32[8,384]{1,0:T(8,128)}) custom-call(s32[1]{0:T(128)} %bitcast.core_ref, f32[8,384]{1,0:T(8,128)} %copy-done.14, f32[8,384]{1,0:T(8,128)} %copy-done.16, f32[16,384]{1,0:T(8,128)} %copy-done.17, bf16[384,1536]{1,0:T(8,128)(2,1)} %q.3, bf16[384,1536]{1,0:T(8,128)(2,1)} %refs_3_.1, ...), custom_call_target="tpu_custom_call" | custom-call | tf_op jit(solution)/shard_map/forward/pallas_call | solution.py:310
  146.6 1.4 collective-permute-done.9.refs_9_
  148.0 1.8 collective-permute-start.11
  151.7 2.7 %collective-permute-done.10.rest_1_ = f32[8,384]{1,0:T(8,128)S(1)} collective-permute-done((f32[8,384]{1,0:T(8,128)}, f32[8,384]{1,0:T(8,128)S(1)}, u32[]{:S(2)}, u32[]{:S(2)}) %collective-permute-start.10) | collective-permute-done | bytes 12320 | tf_op jit(solution)/shard_map/ppermute | solution.py:335
  154.5 10.9 %collective-permute-start.15 = (bf16[384,896]{1,0:T(8,128)(2,1)S(1)}, bf16[384,896]{1,0:T(8,128)(2,1)S(1)}, u32[]{:S(2)}, u32[]{:S(2)}) collective-permute-start(bf16[384,896]{1,0:T(8,128)(2,1)S(1)} %slice.13), channel_id=1, source_target_pairs={{8,0},{12,4},{16,8},{20,12},{24,16},{28,20},{32,24},{36,28},{40,32... | collective-permute-start | bytes 2064392 | tf_op jit(solution)/shard_map/ppermute | solution.py:24
  165.4 9.3 %norm.1 = (bf16[384,1536]{1,0:T(8,128)(2,1)}, f32[32,384]{1,0:T(8,128)}, bf16[384,896]{1,0:T(8,128)(2,1)}, bf16[384,768]{1,0:T(8,128)(2,1)}) custom-call(f32[8,384]{1,0:T(8,128)} %copy-done.14, f32[16,384]{1,0:T(8,128)} %get-tuple-element.56.lse, f32[384,1536]{1,0:T(8,128)} %get-tuple-element.57.o, bf16[384,1536]{1,0:T(8,128)(2,1)} %cot.3, ...), custom_call_target="tpu_custom_call" | custom-call | tf_op jit(solution)/shard_map/norm/pallas_call | solution.py:341
  174.7 1.9 collective-permute-start.14
  176.6 20.3 %own.1 = (bf16[384,1536]{1,0:T(8,128)(2,1)}, f32[384,1536]{1,0:T(8,128)}, f32[384,1536]{1,0:T(8,128)}) custom-call(s32[1]{0:T(128)} %bitcast.core_ref, f32[8,384]{1,0:T(8,128)} %copy-done.14, f32[8,384]{1,0:T(8,128)} %copy-done.16, f32[16,384]{1,0:T(8,128)} %copy-done.17, f32[32,384]{1,0:T(8,128)} %get-tuple-element.67.stats, bf16[384,1536]{1,0:T(8,128)(2,1)} %q.3, ...), custom_call_target="tpu_custom_call" | custom-call | tf_op jit(solution)/shard_map/own/pallas_call | solution.py:358
  197.0 1.3 collective-permute-start.17
  198.3 1.3 collective-permute-start.16
  199.6 14.4 %collective-permute-start.13 = (bf16[384,896]{1,0:T(8,128)(2,1)S(1)}, bf16[384,896]{1,0:T(8,128)(2,1)S(1)}, u32[]{:S(2)}, u32[]{:S(2)}) collective-permute-start(bf16[384,896]{1,0:T(8,128)(2,1)S(1)} %copy-done.11), channel_id=1, source_target_pairs={{4,0},{12,8},{20,16},{28,24},{36,32},{44,40},{52,48},{60,56},{68,6... | collective-permute-start | bytes 2064392 | tf_op jit(solution)/shard_map/ppermute | solution.py:24
  214.0 11.4 %collective-permute-start.21 = (bf16[384,768]{1,0:T(8,128)(2,1)}, bf16[384,768]{1,0:T(8,128)(2,1)}, u32[]{:S(2)}, u32[]{:S(2)}) collective-permute-start(bf16[384,768]{1,0:T(8,128)(2,1)} %get-tuple-element.69.rest_1_), channel_id=1, source_target_pairs={{8,0},{12,4},{16,8},{20,12},{24,16},{28,20},{32,24},{36,28},{40,32... | collective-permute-start | bytes 1769480 | tf_op jit(solution)/shard_map/ppermute | solution.py:24
  225.4 7.7 %collective-permute-done.14.refs_3_.refs_12_ = bf16[384,896]{1,0:T(8,128)(2,1)S(1)} collective-permute-done((bf16[384,896]{1,0:T(8,128)(2,1)}, bf16[384,896]{1,0:T(8,128)(2,1)S(1)}, u32[]{:S(2)}, u32[]{:S(2)}) %collective-permute-start.14) | collective-permute-done | bytes 688160 | tf_op jit(solution)/shard_map/ppermute | solution.py:24
  233.9 1.3 collective-permute-start.18
  235.3 1.3 collective-permute-start.19
  236.6 7.6 %collective-permute-start.20 = (bf16[384,768]{1,0:T(8,128)(2,1)}, bf16[384,768]{1,0:T(8,128)(2,1)}, u32[]{:S(2)}, u32[]{:S(2)}) collective-permute-start(bf16[384,768]{1,0:T(8,128)(2,1)} %get-tuple-element.69.rest_1_), channel_id=1, source_target_pairs={{4,0},{12,8},{20,16},{28,24},{36,32},{44,40},{52,48},{60,56},{68,6... | collective-permute-start | bytes 1769480 | tf_op jit(solution)/shard_map/ppermute | solution.py:24
  245.7 9.4 %keys.2 = (bf16[384,1536]{1,0:T(8,128)(2,1)}, bf16[384,1536]{1,0:T(8,128)(2,1)}, f32[2,384,384]{2,1,0:T(8,128)}, f32[32,384]{1,0:T(8,128)}, f32[32,384]{1,0:T(8,128)}) custom-call(s32[1]{0:T(128)} %bitcast.core_ref, f32[8,384]{1,0:T(8,128)} %copy-done.14, bf16[384,896]{1,0:T(8,128)(2,1)} %copy-done.9, bf16[384,512]{1,0:T(8,128)(2,1)} %copy-done.10, ...), custom_call_target="tpu_custom_call" | custom-call | tf_op jit(solution)/shard_map/keys/pallas_call | solution.py:392
  255.0 1.3 collective-permute-start.22
  256.4 2.8 %collective-permute-done.22.refs_10_ = bf16[384,768]{1,0:T(8,128)(2,1)S(1)} collective-permute-done((bf16[384,768]{1,0:T(8,128)(2,1)}, bf16[384,768]{1,0:T(8,128)(2,1)S(1)}, u32[]{:S(2)}, u32[]{:S(2)}) %collective-permute-start.22) | collective-permute-done | bytes 589856 | tf_op jit(solution)/shard_map/ppermute | solution.py:24
  260.0 9.3 %keys.3 = (bf16[384,1536]{1,0:T(8,128)(2,1)}, bf16[384,1536]{1,0:T(8,128)(2,1)}) custom-call(s32[1]{0:T(128)} %bitcast.core_ref, f32[2,384,384]{2,1,0:T(8,128)} %get-tuple-element.78.refs_0_, f32[32,384]{1,0:T(8,128)} %get-tuple-element.79.refs_1_, f32[32,384]{1,0:T(8,128)} %get-tuple-element.80.refs_2_, ...), custom_call_target="tpu_custom_call", output_to_operand_aliasing={{0}: (14, {}), {1}: (15, {})} | custom-call | tf_op jit(solution)/shard_map/keys/pallas_call | solution.py:413
  (71 shorter events, 11.2 us)
Async XLA Ops:
  0.6 44.6 %collective-permute-start.3 = (bf16[384,1536]{1,0:T(8,128)(2,1)}, bf16[384,1536]{1,0:T(8,128)(2,1)S(1)}, u32[]{:S(2)}, u32[]{:S(2)}) collective-permute-start(bf16[384,1536]{1,0:T(8,128)(2,1)} %refs_3_.1), channel_id=1, source_target_pairs={{0,8},{4,12},{8,16},{12,20},{16,24},{20,28},{24,32},{28,36},{32,40... | collective-permute-start | bytes 3538952 | tf_op jit(solution)/shard_map/ppermute | solution.py:24
  10.1 45.7 %copy-start.14 = (f32[8,384]{1,0:T(8,128)}, f32[8,384]{1,0:T(8,128)S(1)}, u32[]{:S(2)}) copy-start(f32[8,384]{1,0:T(8,128)S(1)} %broadcast_in_dim.2.d0.docs.refs_0_) | copy-start | bytes 36868
  10.2 1.8 collective-permute-start.1
  11.9 40.2 %copy-start.16 = (f32[8,384]{1,0:T(8,128)}, f32[8,384]{1,0:T(8,128)S(1)}, u32[]{:S(2)}) copy-start(f32[8,384]{1,0:T(8,128)S(1)} %collective-permute-done.1.d1) | copy-start | bytes 36868
  11.9 43.9 %copy-start.21 = (f32[1536]{0:T(1024)S(1)}, f32[1536]{0:T(1024)}, u32[]{:S(2)}) copy-start(f32[1536]{0:T(1024)} %param.11) | copy-start | bytes 18436
  11.9 40.2 %collective-permute-start.2 = (f32[16,384]{1,0:T(8,128)S(1)}, f32[16,384]{1,0:T(8,128)S(1)}, u32[]{:S(2)}, u32[]{:S(2)}) collective-permute-start(f32[16,384]{1,0:T(8,128)S(1)} %pad_maximum_fusion), channel_id=1, source_target_pairs={{0,8},{4,12},{8,16},{12,20},{16,24},{20,28},{24,32},{28,36},{32,40... | collective-permute-start | bytes 73736 | tf_op jit(solution)/shard_map/ppermute | solution.py:24
  14.0 69.9 %collective-permute-start = (bf16[384,1536]{1,0:T(8,128)(2,1)}, bf16[384,1536]{1,0:T(8,128)(2,1)}, u32[]{:S(2)}, u32[]{:S(2)}) collective-permute-start(bf16[384,1536]{1,0:T(8,128)(2,1)} %refs_4_.3), channel_id=1, source_target_pairs={{0,8},{4,12},{8,16},{12,20},{16,24},{20,28},{24,32},{28,36},{32,40... | collective-permute-start | bytes 3538952 | tf_op jit(solution)/shard_map/ppermute | solution.py:24
  45.2 38.7 %collective-permute-start.5 = (bf16[384,1536]{1,0:T(8,128)(2,1)}, bf16[384,1536]{1,0:T(8,128)(2,1)S(1)}, u32[]{:S(2)}, u32[]{:S(2)}) collective-permute-start(bf16[384,1536]{1,0:T(8,128)(2,1)} %refs_3_.1), channel_id=1, source_target_pairs={{0,4},{8,12},{16,20},{24,28},{32,36},{40,44},{48,52},{56,60},{64,6... | collective-permute-start | bytes 3538952 | tf_op jit(solution)/shard_map/ppermute | solution.py:24
  46.5 37.4 %collective-permute-start.6 = (bf16[384,1536]{1,0:T(8,128)(2,1)}, bf16[384,1536]{1,0:T(8,128)(2,1)S(1)}, u32[]{:S(2)}, u32[]{:S(2)}) collective-permute-start(bf16[384,1536]{1,0:T(8,128)(2,1)} %refs_4_.3), channel_id=1, source_target_pairs={{0,4},{8,12},{16,20},{24,28},{32,36},{40,44},{48,52},{56,60},{64,6... | collective-permute-start | bytes 3538952 | tf_op jit(solution)/shard_map/ppermute | solution.py:24
  47.8 36.1 %collective-permute-start.7 = (bf16[384,1536]{1,0:T(8,128)(2,1)}, bf16[384,1536]{1,0:T(8,128)(2,1)S(1)}, u32[]{:S(2)}, u32[]{:S(2)}) collective-permute-start(bf16[384,1536]{1,0:T(8,128)(2,1)} %q.3), channel_id=1, source_target_pairs={{4,0},{12,8},{20,16},{28,24},{36,32},{44,40},{52,48},{60,56},{68,6... | collective-permute-start | bytes 3538952 | tf_op jit(solution)/shard_map/ppermute | solution.py:24
  52.2 31.7 %collective-permute-start.4 = (bf16[384,1536]{1,0:T(8,128)(2,1)S(1)}, bf16[384,1536]{1,0:T(8,128)(2,1)S(1)}, u32[]{:S(2)}, u32[]{:S(2)}) collective-permute-start(bf16[384,1536]{1,0:T(8,128)(2,1)S(1)} %collective-permute-done.3.k2), channel_id=1, source_target_pairs={{4,0},{12,8},{20,16},{28,24},{36,32},{44,40},{52,48},{60,56},{68,6... | collective-permute-start | bytes 3538952 | tf_op jit(solution)/shard_map/ppermute | solution.py:24
  83.9 32.3 %copy-start.4 = (bf16[384,1536]{1,0:T(8,128)(2,1)}, bf16[384,1536]{1,0:T(8,128)(2,1)S(1)}, u32[]{:S(2)}) copy-start(bf16[384,1536]{1,0:T(8,128)(2,1)S(1)} %collective-permute-done.6.vc) | copy-start | bytes 3538948
  83.9 62.7 %copy-start.1 = (bf16[384,1536]{1,0:T(8,128)(2,1)}, bf16[384,1536]{1,0:T(8,128)(2,1)S(1)}, u32[]{:S(2)}) copy-start(bf16[384,1536]{1,0:T(8,128)(2,1)S(1)} %collective-permute-done.7.refs_6_.refs_5_) | copy-start | bytes 3538948
  84.9 41.8 %copy-start.5 = (bf16[384,1536]{1,0:T(8,128)(2,1)}, bf16[384,1536]{1,0:T(8,128)(2,1)S(1)}, u32[]{:S(2)}) copy-start(bf16[384,1536]{1,0:T(8,128)(2,1)S(1)} %collective-permute-done.4.kd) | copy-start | bytes 3538948
  84.9 41.9 %collective-permute-start.8 = (bf16[384,1536]{1,0:T(8,128)(2,1)}, bf16[384,1536]{1,0:T(8,128)(2,1)S(1)}, u32[]{:S(2)}, u32[]{:S(2)}) collective-permute-start(bf16[384,1536]{1,0:T(8,128)(2,1)} %collective-permute-done.v2), channel_id=1, source_target_pairs={{4,0},{12,8},{20,16},{28,24},{36,32},{44,40},{52,48},{60,56},{68,6... | collective-permute-start | bytes 3538952 | tf_op jit(solution)/shard_map/ppermute | solution.py:24
  116.2 31.8 %collective-permute-start.9 = (bf16[384,640]{1,0:T(8,128)(2,1)S(1)}, bf16[384,640]{1,0:T(8,128)(2,1)}, u32[]{:S(2)}, u32[]{:S(2)}) collective-permute-start(bf16[384,640]{1,0:T(8,128)(2,1)S(1)} %slice.12), channel_id=1, source_target_pairs={{8,0},{12,4},{16,8},{20,12},{24,16},{28,20},{32,24},{36,28},{40,32... | collective-permute-start | bytes 1474568 | tf_op jit(solution)/shard_map/ppermute | solution.py:24
  148.0 2.8 %collective-permute-start.12 = (f32[8,384]{1,0:T(8,128)}, f32[8,384]{1,0:T(8,128)S(1)}, u32[]{:S(2)}, u32[]{:S(2)}) collective-permute-start(f32[8,384]{1,0:T(8,128)} %get-tuple-element.62.rest_0_), channel_id=1, source_target_pairs={{0,3},{1,0},{2,1},{3,2},{4,7},{5,4},{6,5},{7,6},{8,11},{9,8},{10,9... | collective-permute-start | bytes 36872 | tf_op jit(solution)/shard_map/ppermute | solution.py:335
  148.0 3.7 %collective-permute-start.11 = (f32[8,384]{1,0:T(8,128)}, f32[8,384]{1,0:T(8,128)S(1)}, u32[]{:S(2)}, u32[]{:S(2)}) collective-permute-start(f32[8,384]{1,0:T(8,128)} %get-tuple-element.62.rest_0_), channel_id=1, source_target_pairs={{0,2},{1,3},{2,0},{3,1},{4,6},{5,7},{6,4},{7,5},{8,10},{9,11},{10,... | collective-permute-start | bytes 36872 | tf_op jit(solution)/shard_map/ppermute | solution.py:335
  149.9 4.6 %collective-permute-start.10 = (f32[8,384]{1,0:T(8,128)}, f32[8,384]{1,0:T(8,128)S(1)}, u32[]{:S(2)}, u32[]{:S(2)}) collective-permute-start(f32[8,384]{1,0:T(8,128)} %get-tuple-element.62.rest_0_), channel_id=1, source_target_pairs={{0,1},{1,2},{2,3},{3,0},{4,5},{5,6},{6,7},{7,4},{8,9},{9,10},{10,1... | collective-permute-start | bytes 36872 | tf_op jit(solution)/shard_map/ppermute | solution.py:335
  150.8 14.6 %copy-start.18 = (f32[8,384]{1,0:T(8,128)}, f32[8,384]{1,0:T(8,128)S(1)}, u32[]{:S(2)}) copy-start(f32[8,384]{1,0:T(8,128)S(1)} %collective-permute-done.12.rest_3_) | copy-start | bytes 36868
  154.5 42.5 %collective-permute-start.15 = (bf16[384,896]{1,0:T(8,128)(2,1)S(1)}, bf16[384,896]{1,0:T(8,128)(2,1)S(1)}, u32[]{:S(2)}, u32[]{:S(2)}) collective-permute-start(bf16[384,896]{1,0:T(8,128)(2,1)S(1)} %slice.13), channel_id=1, source_target_pairs={{8,0},{12,4},{16,8},{20,12},{24,16},{28,20},{32,24},{36,28},{40,32... | collective-permute-start | bytes 2064392 | tf_op jit(solution)/shard_map/ppermute | solution.py:24
  174.7 58.4 %collective-permute-start.14 = (bf16[384,896]{1,0:T(8,128)(2,1)}, bf16[384,896]{1,0:T(8,128)(2,1)S(1)}, u32[]{:S(2)}, u32[]{:S(2)}) collective-permute-start(bf16[384,896]{1,0:T(8,128)(2,1)} %get-tuple-element.68.rest_0_), channel_id=1, source_target_pairs={{8,0},{12,4},{16,8},{20,12},{24,16},{28,20},{32,24},{36,28},{40,32... | collective-permute-start | bytes 2064392 | tf_op jit(solution)/shard_map/ppermute | solution.py:24
  176.6 23.0 %copy-start.11 = (bf16[384,896]{1,0:T(8,128)(2,1)S(1)}, bf16[384,896]{1,0:T(8,128)(2,1)}, u32[]{:S(2)}) copy-start(bf16[384,896]{1,0:T(8,128)(2,1)} %get-tuple-element.68.rest_0_) | copy-start | bytes 2064388
  197.0 48.0 %copy-start.7 = (bf16[384,896]{1,0:T(8,128)(2,1)}, bf16[384,896]{1,0:T(8,128)(2,1)S(1)}, u32[]{:S(2)}) copy-start(bf16[384,896]{1,0:T(8,128)(2,1)S(1)} %collective-permute-done.15.refs_10_.refs_7_) | copy-start | bytes 2064388
  197.0 36.1 %collective-permute-start.17 = (bf16[384,896]{1,0:T(8,128)(2,1)S(1)}, bf16[384,896]{1,0:T(8,128)(2,1)S(1)}, u32[]{:S(2)}, u32[]{:S(2)}) collective-permute-start(bf16[384,896]{1,0:T(8,128)(2,1)S(1)} %collective-permute-done.15.refs_10_.refs_7_), channel_id=1, source_target_pairs={{0,4},{8,12},{16,20},{24,28},{32,36},{40,44},{48,52},{56,60},{64,6... | collective-permute-start | bytes 2064392 | tf_op jit(solution)/shard_map/ppermute | solution.py:24
  198.3 34.8 %collective-permute-start.16 = (bf16[384,640]{1,0:T(8,128)(2,1)}, bf16[384,640]{1,0:T(8,128)(2,1)S(1)}, u32[]{:S(2)}, u32[]{:S(2)}) collective-permute-start(bf16[384,640]{1,0:T(8,128)(2,1)} %collective-permute-done.9.refs_9_), channel_id=1, source_target_pairs={{0,4},{8,12},{16,20},{24,28},{32,36},{40,44},{48,52},{56,60},{64,6... | collective-permute-start | bytes 1474568 | tf_op jit(solution)/shard_map/ppermute | solution.py:24
  199.6 44.6 %collective-permute-start.13 = (bf16[384,896]{1,0:T(8,128)(2,1)S(1)}, bf16[384,896]{1,0:T(8,128)(2,1)S(1)}, u32[]{:S(2)}, u32[]{:S(2)}) collective-permute-start(bf16[384,896]{1,0:T(8,128)(2,1)S(1)} %copy-done.11), channel_id=1, source_target_pairs={{4,0},{12,8},{20,16},{28,24},{36,32},{44,40},{52,48},{60,56},{68,6... | collective-permute-start | bytes 2064392 | tf_op jit(solution)/shard_map/ppermute | solution.py:24
  214.0 41.1 %collective-permute-start.21 = (bf16[384,768]{1,0:T(8,128)(2,1)}, bf16[384,768]{1,0:T(8,128)(2,1)}, u32[]{:S(2)}, u32[]{:S(2)}) collective-permute-start(bf16[384,768]{1,0:T(8,128)(2,1)} %get-tuple-element.69.rest_1_), channel_id=1, source_target_pairs={{8,0},{12,4},{16,8},{20,12},{24,16},{28,20},{32,24},{36,28},{40,32... | collective-permute-start | bytes 1769480 | tf_op jit(solution)/shard_map/ppermute | solution.py:24
  233.9 10.2 %collective-permute-start.18 = (bf16[384,512]{1,0:T(8,128)(2,1)S(1)}, bf16[384,512]{1,0:T(8,128)(2,1)S(1)}, u32[]{:S(2)}, u32[]{:S(2)}) collective-permute-start(bf16[384,512]{1,0:T(8,128)(2,1)S(1)} %slice.14), channel_id=1, source_target_pairs={{0,4},{8,12},{16,20},{24,28},{32,36},{40,44},{48,52},{56,60},{64,6... | collective-permute-start | bytes 1179656 | tf_op jit(solution)/shard_map/ppermute | solution.py:24
  235.3 8.9 %collective-permute-start.19 = (bf16[384,384]{1,0:T(8,128)(2,1)S(1)}, bf16[384,384]{1,0:T(8,128)(2,1)S(1)}, u32[]{:S(2)}, u32[]{:S(2)}) collective-permute-start(bf16[384,384]{1,0:T(8,128)(2,1)S(1)} %slice.15), channel_id=1, source_target_pairs={{0,4},{8,12},{16,20},{24,28},{32,36},{40,44},{48,52},{56,60},{64,6... | collective-permute-start | bytes 884744 | tf_op jit(solution)/shard_map/ppermute | solution.py:24
  236.6 19.8 %collective-permute-start.20 = (bf16[384,768]{1,0:T(8,128)(2,1)}, bf16[384,768]{1,0:T(8,128)(2,1)}, u32[]{:S(2)}, u32[]{:S(2)}) collective-permute-start(bf16[384,768]{1,0:T(8,128)(2,1)} %get-tuple-element.69.rest_1_), channel_id=1, source_target_pairs={{4,0},{12,8},{20,16},{28,24},{36,32},{44,40},{52,48},{60,56},{68,6... | collective-permute-start | bytes 1769480 | tf_op jit(solution)/shard_map/ppermute | solution.py:24
  255.0 4.1 %collective-permute-start.22 = (bf16[384,768]{1,0:T(8,128)(2,1)}, bf16[384,768]{1,0:T(8,128)(2,1)S(1)}, u32[]{:S(2)}, u32[]{:S(2)}) collective-permute-start(bf16[384,768]{1,0:T(8,128)(2,1)} %collective-permute-done.21.refs_9_), channel_id=1, source_target_pairs={{0,4},{8,12},{16,20},{24,28},{32,36},{40,44},{48,52},{56,60},{64,6... | collective-permute-start | bytes 1769480 | tf_op jit(solution)/shard_map/ppermute | solution.py:24
  (13 other events, 69.1 us)
